TPU v7x, 128 devices: a whole 4x4x4 slice. The times are simulated.
128 devices in a mesh: outer: 16 (over x_hi, z, core), inner: 8 (over y, x_lo).
Axes of the slice: x: 4 (x_hi: 2, x_lo: 2; x = x_hi * 2 + x_lo), y: 4, z: 4, core: 2. Of those that a mesh axis runs over, the one named last changes fastest.
Arguments:
- queries: bfloat16 [16384, 2048], P(('outer', 'inner')), may hold values from -80 to 80
- key_vals: bfloat16 [16384, 512], P(('outer', 'inner')), may hold values from -6 to 6
- key_block_scale: bfloat16 [16384, 4], P(('outer', 'inner')), may hold values from 0.5 to 2
- stored_value_entries: bfloat16 [16384, 512], P(('outer', 'inner')), may hold values from -6 to 6
- value_block_scale: bfloat16 [16384, 4], P(('outer', 'inner')), may hold values from 0.5 to 2
- span_pos: int32 [256], P(('outer', 'inner')), may hold values from 0 to 255, each once
- page_of_slot: int32 [256], P(('outer', 'inner')), may hold values from 0 to 255, each once
Outputs:
- attended: bfloat16 [16384, 2048], P(('outer', 'inner'))
- slot_page_keys: bfloat16 [256, 64, 512], P(('outer', 'inner'))
- slot_page_values: bfloat16 [256, 64, 512], P(('outer', 'inner'))
Inputs may be any that keep to these rules, and one draw needn't show every extreme that they name: `span_pos`: each span position occurs exactly once. `page_of_slot`: each page occurs exactly once.
All inputs are finite; a program needn't handle non-finite values.
Results may differ from a plain program's by a relative error of at most 0.0077.
Values may be sent and summed in bfloat16 or wider, within the bound.
No kernel may reach another device: no remote copies, remote signals or barrier semaphores. Data moves between devices by JAX's collectives and lax.ppermute only.
A program may use at most 384 MiB of HBM per device.

v0:
```python
import math

import jax
import jax.numpy as jnp
from jax import lax
from jax.sharding import PartitionSpec as P


def local(
    queries,
    key_vals,
    key_block_scale,
    stored_value_entries,
    value_block_scale,
    span_pos,
    page_of_slot,
):
    tok_rows = queries.shape[0]
    kv_heads = key_block_scale.shape[1]
    head_size = key_vals.shape[1] // kv_heads
    query_groups = queries.shape[1] // (kv_heads * head_size)
    span_len = tok_rows // span_pos.shape[0]
    factor = 1.0 / math.sqrt(head_size)
    query_pos = (
        span_pos[:, None] * span_len + jnp.arange(span_len, dtype=jnp.int32)[None, :]
    ).reshape(-1)
    query_four = queries.reshape(tok_rows, kv_heads, query_groups, head_size)

    def dequantize(value_entries, scales):
        count = value_entries.shape[0]
        reshaped_array = value_entries.astype(jnp.float32).reshape(count, kv_heads, head_size)
        return (reshaped_array * scales.astype(jnp.float32)[:, :, None]).astype(jnp.bfloat16)

    start_state = (
        jnp.full((kv_heads, query_groups, tok_rows), -1e30, jnp.float32),
        jnp.zeros((kv_heads, query_groups, tok_rows), jnp.float32),
        jnp.zeros((kv_heads, query_groups, tok_rows, head_size), jnp.float32),
    )
    grouped = (
        lax.all_gather(key_vals, "inner", axis=0, tiled=True),
        lax.all_gather(key_block_scale, "inner", axis=0, tiled=True),
        lax.all_gather(stored_value_entries, "inner", axis=0, tiled=True),
        lax.all_gather(value_block_scale, "inner", axis=0, tiled=True),
        lax.all_gather(span_pos, "inner", axis=0, tiled=True),
    )
    current = start_state
    piece_k = lax.all_gather(grouped[0], "outer", axis=0, tiled=True)
    piece_ks = lax.all_gather(grouped[1], "outer", axis=0, tiled=True)
    piece_v = lax.all_gather(grouped[2], "outer", axis=0, tiled=True)
    piece_vs = lax.all_gather(grouped[3], "outer", axis=0, tiled=True)
    piece_pos = lax.all_gather(grouped[4], "outer", axis=0, tiled=True)
    spans_in = piece_pos.shape[0]
    key_rows = dequantize(piece_k, piece_ks)
    value_rows = dequantize(piece_v, piece_vs)
    key_pos = (
        piece_pos[:, None] * span_len + jnp.arange(span_len, dtype=jnp.int32)[None, :]
    ).reshape(-1)
    running, totals, outputs = current
    raw_scores = jnp.einsum(
        "qhgd,khd->hgqk", query_four, key_rows, preferred_element_type=jnp.float32
    )
    visible = key_pos[None, :] <= query_pos[:, None]
    piece_max = jnp.max(jnp.where(visible, raw_scores, -1e30), axis=-1) * factor
    new_max = jnp.maximum(running, piece_max)
    weights = jnp.where(visible, jnp.exp(raw_scores * factor - new_max[..., None]), 0.0)
    totals = jnp.sum(weights, axis=-1)
    product = jnp.einsum(
        "hgqk,khd->hgqd",
        weights.astype(jnp.bfloat16),
        value_rows,
        preferred_element_type=jnp.float32,
    )
    outputs = product
    current = (new_max, totals, outputs)
    select = (piece_pos[None, :] == page_of_slot[:, None]).astype(jnp.bfloat16)
    cache_k = jnp.einsum(
        "sc,crw->srw",
        select,
        key_rows.reshape(spans_in, span_len, kv_heads * head_size),
        preferred_element_type=jnp.float32,
    )
    cache_v = jnp.einsum(
        "sc,crw->srw",
        select,
        value_rows.reshape(spans_in, span_len, kv_heads * head_size),
        preferred_element_type=jnp.float32,
    )
    result = (current, cache_k, cache_v)
    final_state, cache_k, cache_v = result
    outputs = final_state[2] / final_state[1][..., None]
    attended = (
        jnp.transpose(outputs, (2, 0, 1, 3))
        .reshape(tok_rows, kv_heads * query_groups * head_size)
        .astype(jnp.bfloat16)
    )
    return (attended, cache_k.astype(jnp.bfloat16), cache_v.astype(jnp.bfloat16))


def solution(mesh):
    in_specs = (
        P(("outer", "inner"), None),
        P(("outer", "inner"), None),
        P(("outer", "inner"), None),
        P(("outer", "inner"), None),
        P(("outer", "inner"), None),
        P(("outer", "inner")),
        P(("outer", "inner")),
    )
    out_specs = (
        P(("outer", "inner"), None),
        P(("outer", "inner"), None, None),
        P(("outer", "inner"), None, None),
    )
    return jax.shard_map(local, mesh=mesh, in_specs=in_specs, out_specs=out_specs, check_vma=False)
```

profile of v0, /device:TPU:1, one launch (start us, length us, event | category | flops | bytes accessed | tf_op | source)
XLA Modules:
  0.0 769.6 jit_solution(5982369425633895034)
XLA Ops:
  8.7 39.9 %all-gather.9.cloned.1.call-done = bf16[1024,512]{1,0:T(8,128)(2,1)} async-done(((bf16[128,512]{1,0:T(8,128)(2,1)}), bf16[1024,512]{1,0:T(8,128)(2,1)}) %all-gather.9.cloned.1.call-update) | async-done | bytes 1048592 | tf_op jit(solution)/shard_map/all_gather | solution.py:42
  48.7 41.5 %all-gather.5.cloned.1.call-done = bf16[1024,512]{1,0:T(8,128)(2,1)} async-done(((bf16[128,512]{1,0:T(8,128)(2,1)}), bf16[1024,512]{1,0:T(8,128)(2,1)}) %all-gather.5.cloned.1.call-update) | async-done | bytes 1048592 | tf_op jit(solution)/shard_map/all_gather | solution.py:40
  102.8 20.4 %all-reduce.1 = s32[256]{0:T(256)S(1)} all-reduce(s32[256]{0:T(256)S(1)} %dynamic-update-slice.1), channel_id=1, replica_groups=mesh['outer'=16,'inner'=8] {'outer'}, use_global_device_ids=true, to_apply=%add.1 | all-reduce | flops 256 | bytes 2048
  125.6 12.7 %all_gather.34 = bf16[1024,4]{0,1:T(4,128)(2,1)S(1)} all-gather(bf16[128,4]{0,1:T(4,128)(2,1)} %param.9), channel_id=1, replica_groups=mesh['outer'=16,'inner'=8] {'inner'}, dimensions={0}, use_global_device_ids=true | all-gather | bytes 9216 | tf_op jit(solution)/shard_map/all_gather | solution.py:41
  138.3 27.5 %all_gather.35 = bf16[16384,4]{0,1:T(4,128)(2,1)S(1)} all-gather(bf16[1024,4]{0,1:T(4,128)(2,1)S(1)} %all_gather.34), channel_id=1, replica_groups=mesh['outer'=16,'inner'=8] {'outer'}, dimensions={0}, use_global_device_ids=true | all-gather | bytes 139264 | tf_op jit(solution)/shard_map/all_gather | solution.py:48
  170.0 13.1 %all_gather.38 = bf16[1024,4]{0,1:T(4,128)(2,1)S(1)} all-gather(bf16[128,4]{0,1:T(4,128)(2,1)} %param.11), channel_id=1, replica_groups=mesh['outer'=16,'inner'=8] {'inner'}, dimensions={0}, use_global_device_ids=true | all-gather | bytes 9216 | tf_op jit(solution)/shard_map/all_gather | solution.py:43
  183.1 23.4 %all_gather.39 = bf16[16384,4]{0,1:T(4,128)(2,1)S(1)} all-gather(bf16[1024,4]{0,1:T(4,128)(2,1)S(1)} %all_gather.38), channel_id=1, replica_groups=mesh['outer'=16,'inner'=8] {'outer'}, dimensions={0}, use_global_device_ids=true | all-gather | bytes 139264 | tf_op jit(solution)/shard_map/all_gather | solution.py:50
  210.8 31.3 %mul.62 = f32[16384,4,128]{2,1,0:T(4,128)} broadcast(f32[16384,4]{1,0:T(8,128)} %copy.22), dimensions={0,1} | broadcast | bytes 33816576 | tf_op jit(solution)/shard_map/mul | solution.py:32
  242.2 38.7 %mul.66 = f32[256,64,512]{2,1,0:T(8,128)} reshape(f32[16384,4,128]{2,1,0:T(4,128)} %mul.62) | data formatting | bytes 67108864 | tf_op jit(solution)/shard_map/mul | solution.py:32
  280.9 31.3 %mul.56 = f32[16384,4,128]{2,1,0:T(4,128)} broadcast(f32[16384,4]{1,0:T(8,128)} %copy.19), dimensions={0,1} | broadcast | bytes 33816576 | tf_op jit(solution)/shard_map/mul | solution.py:32
  312.2 39.2 %mul.64 = f32[256,64,512]{2,1,0:T(8,128)} reshape(f32[16384,4,128]{2,1,0:T(4,128)} %mul.56) | data formatting | bytes 67108864 | tf_op jit(solution)/shard_map/mul | solution.py:32
  358.8 18.9 %convert_element_type.44 = f32[16384,512]{1,0:T(8,128)} convert(bf16[16384,512]{1,0:T(8,128)(2,1)} %all-gather.11.cloned.1.call-done) | non-fusion elementwise | flops 8388608 | bytes 50331648 | tf_op jit(solution)/shard_map/convert_element_type | solution.py:31
  377.7 28.1 %multiply_convert_fusion = bf16[256,64,512]{2,1,0:T(8,128)(2,1)} fusion(f32[256,64,512]{2,1,0:T(8,128)} %bitcast.40, f32[256,64,512]{2,1,0:T(8,128)} %mul.66), kind=kLoop, calls=%fused_computation.10 | loop fusion | flops 16777216 | bytes 83886080 | tf_op jit(solution)/shard_map/convert_element_type | solution.py:32
  405.8 23.4 %fusion.26 = bf16[2,64,512]{2,0,1:T(2,128)(2,1)S(1)} fusion(bf16[256,64,512]{2,1,0:T(8,128)(2,1)} %multiply_convert_fusion, s32[256]{0:T(256)S(1)} %all-reduce.1, s32[2]{0:T(128)S(1)} %copy-done.2), kind=kOutput, calls=%fused_computation.26 | convolution fusion | flops 33620480 | bytes 16909320 | tf_op jit(solution)/shard_map/sc,crw->srw/dot_general | solution.py:82
  429.9 29.7 %reshape.70 = f32[16384,4,128]{2,1,0:T(4,128)} reshape(bf16[16384,512]{1,0:T(8,128)(2,1)} %all-gather.11.cloned.1.call-done) | data formatting | bytes 50331648 | tf_op jit(solution)/shard_map/reshape | solution.py:31
  459.6 33.2 %fusion.10 = bf16[16384,4,128,1]{2,1,0,3:T(4,128)(2,1)} fusion(f32[16384,4,128]{2,1,0:T(4,128)} %reshape.70, f32[16384,4]{1,0:T(8,128)} %copy.22), kind=kLoop, calls=%fused_computation.15 | loop fusion | flops 16777216 | bytes 50593792 | tf_op jit(solution)/shard_map/convert_element_type | solution.py:32
  492.9 29.7 %reshape.68 = f32[16384,4,128]{2,1,0:T(4,128)} reshape(bf16[16384,512]{1,0:T(8,128)(2,1)} %all-gather.7.cloned.1.call-done) | data formatting | bytes 50331648 | tf_op jit(solution)/shard_map/reshape | solution.py:31
  522.6 33.4 %fusion.9 = bf16[16384,4,128,1]{2,1,0,3:T(4,128)(2,1)} fusion(f32[16384,4,128]{2,1,0:T(4,128)} %reshape.68, f32[16384,4]{1,0:T(8,128)} %copy.19), kind=kLoop, calls=%fused_computation.14 | loop fusion | flops 16777216 | bytes 50593792 | tf_op jit(solution)/shard_map/convert_element_type | solution.py:32
  556.0 12.4 %convert_element_type.40 = f32[16384,512]{1,0:T(8,128)} convert(bf16[16384,512]{1,0:T(8,128)(2,1)S(1)} %copy-done) | non-fusion elementwise | flops 8388608 | bytes 50331648 | tf_op jit(solution)/shard_map/convert_element_type | solution.py:31
  568.4 27.9 %multiply_convert_fusion.1 = bf16[256,64,512]{2,1,0:T(8,128)(2,1)} fusion(f32[256,64,512]{2,1,0:T(8,128)} %bitcast.39, f32[256,64,512]{2,1,0:T(8,128)} %mul.64), kind=kLoop, calls=%fused_computation.11 | loop fusion | flops 16777216 | bytes 83886080 | tf_op jit(solution)/shard_map/convert_element_type | solution.py:32
  596.2 23.6 %fusion.23 = bf16[2,64,512]{2,0,1:T(2,128)(2,1)S(1)} fusion(bf16[256,64,512]{2,1,0:T(8,128)(2,1)} %multiply_convert_fusion.1, s32[256]{0:T(256)S(1)} %all-reduce.1, s32[2]{0:T(128)S(1)} %copy-done.2), kind=kOutput, calls=%fused_computation.25 | convolution fusion | flops 33620480 | bytes 16909320 | tf_op jit(solution)/shard_map/sc,crw->srw/dot_general | solution.py:76
  620.6 51.0 %fusion.3 = (f32[4,4,128]{2,1,0:T(4,128)S(1)}, f32[4,16384,128,4]{2,1,3,0:T(8,128)}) fusion(pred[128,16384]{0,1:T(8,128)(4,1)S(1)} %broadcast_compare_fusion, bf16[128,4,4,128]{3,2,1,0:T(4,128)(2,1)S(1)} %copy-done.1, bf16[16384,4,128,1]{2,1,0,3:T(4,128)(2,1)} %fusion.9), kind=kOutput, calls=%fused_computation.5 | convolution fusion | flops 8657041408 | bytes 153624576 | tf_op jit(solution)/shard_map/qhgd,khd->hgqk/dot_general | solution.py:59
  671.5 41.1 %fusion.4 = f32[4,4,128]{2,1,0:T(4,128)S(1)} fusion(f32[4,16384,128,4]{2,1,3,0:T(8,128)} %get-tuple-element.10, f32[4,4,128]{2,1,0:T(4,128)S(1)} %multiply_maximum_fusion, pred[128,16384]{0,1:T(8,128)(4,1)S(1)} %broadcast_compare_fusion), kind=kLoop, calls=%fused_computation.6 | loop fusion | flops 134215680 | bytes 136331264 | tf_op jit(solution)/shard_map/reduce_sum | solution.py:66
  712.6 49.3 %divide_convert_fusion = bf16[128,4,4,128]{0,3,2,1:T(8,128)(2,1)S(1)} fusion(f32[128,4,4]{0,2,1:T(4,128)S(1)} %bitcast.42, f32[4,16384,128,4]{2,1,3,0:T(8,128)} %get-tuple-element.10, f32[4,4,128]{2,1,0:T(4,128)S(1)} %multiply_maximum_fusion, pred[128,16384]{0,1:T(8,128)(4,1)S(1)} %broadcast_compare_fusion, bf16[16384,4,128,1]{2,1,0,3:T(4,128)(2,1)} %fusion.10), kind=kOutput, calls=%fused_computation.27 | convolution fusion | flops 8724676608 | bytes 153632768 | tf_op jit(solution)/shard_map/hgqk,khd->hgqd/dot_general | solution.py:67
  (37 shorter events, 33.6 us)
Async XLA Ops:
  7.2 41.5 %all-gather.9.cloned.1.call-start = ((), (), s32[]{:S(2)}) async-start(), calls=%async_computation.2 | async-start | bytes 1179648 | tf_op jit(solution)/shard_map/all_gather | solution.py:42
  7.9 82.3 %all-gather.5.cloned.1.call-start = ((), (), s32[]{:S(2)}) async-start(), calls=%async_computation | async-start | bytes 1179648 | tf_op jit(solution)/shard_map/all_gather | solution.py:40
  8.6 350.1 %all-gather.11.cloned.1.call-start = ((), (), s32[]{:S(2)}) async-start(), calls=%async_computation.3 | async-start | bytes 17825792 | tf_op jit(solution)/shard_map/all_gather | solution.py:49
  48.6 444.2 %all-gather.7.cloned.1.call-start = ((), (), s32[]{:S(2)}) async-start(), calls=%async_computation.1 | async-start | bytes 17825792 | tf_op jit(solution)/shard_map/all_gather | solution.py:47
  377.7 28.2 %copy-start.2 = (s32[2]{0:T(128)S(1)}, s32[2]{0:T(128)}, u32[]{:S(2)}) copy-start(s32[2]{0:T(128)} %param.13) | copy-start | bytes 28
  522.6 33.4 %copy-start = (bf16[16384,512]{1,0:T(8,128)(2,1)S(1)}, bf16[16384,512]{1,0:T(8,128)(2,1)}, u32[]{:S(2)}) copy-start(bf16[16384,512]{1,0:T(8,128)(2,1)} %all-gather.7.cloned.1.call-done) | copy-start | bytes 50331652
  568.4 52.2 %copy-start.1 = (bf16[128,4,4,128]{3,2,1,0:T(4,128)(2,1)S(1)}, bf16[128,4,4,128]{3,2,1,0:T(4,128)(2,1)}, u32[]{:S(2)}) copy-start(bf16[128,4,4,128]{3,2,1,0:T(4,128)(2,1)} %reshape.69) | copy-start | bytes 1572868
Sparse Core Ops, SparseCore 0:
  9.6 38.9 all-gather.8
  50.3 39.8 all-gather.4
  92.7 115.3 all-gather.10
  210.4 106.8 all-gather.6
where the time goes:
time: 779 us; the launch traced here: 770 us
  local copies, waits for them, and re-layouts  217 us (28%)
  other arithmetic  203 us (26%)
  matrix products  147 us (19%)
  blocking collectives  104 us (13%)
  waiting for transfers between devices  82.9 us (11%)
  between operations  15.4 us (2%)
    mul x4, local copies, waits for them, and re-layouts, dequantize(): reshaped_array * scales.astype(jnp.float32)[:, :, None]  141 us
    convert_element_type x4, other arithmetic, dequantize(): (reshaped_array * scales.astype(jnp.float32)[:, :, None]).astype(jnp.bflo...  123 us
    reshape x2, local copies, waits for them, and re-layouts, dequantize(): value_entries.astype(jnp.float32).reshape(count, kv_heads, head_size)  59.4 us
    dot_general x1, matrix products, local(): jnp.einsum('qhgd,khd->hgqk', query_four, key_rows, preferred_element_type...  51 us
    dot_general x1, matrix products, local(): jnp.einsum('hgqk,khd->hgqd', weights.astype(jnp.bfloat16), value_rows, pr...  49.3 us
    all_gather x1, waiting for transfers between devices, local(): lax.all_gather(key_vals, 'inner', axis=0, tiled=True)  41.5 us
    reduce_sum x1, other arithmetic, local(): totals = jnp.sum(weights, axis=-1)  41.1 us
    all_gather x1, waiting for transfers between devices, local(): lax.all_gather(stored_value_entries, 'inner', axis=0, tiled=True)  39.9 us
  transfers between devices with their start and end apart: 4, of which 2 were waited for; matrix products, arithmetic and copies ran while one was open for 39% of the time, Pallas kernels for 0%

commit v1 on v0

v1 whole, which is shorter than its diff:
```python
import functools
import math

import jax
import jax.numpy as jnp
from jax import lax
from jax.experimental import pallas as pl
from jax.experimental.pallas import tpu as pltpu
from jax.sharding import Mesh
from jax.sharding import PartitionSpec as P

AXES = ("xh", "z", "c", "y", "xl")
X = ("xh", "xl")
BF16 = jnp.bfloat16
F32 = jnp.float32
SPAN = 64
HEADS = 4
GROUP = 4
D = 128
ROWS = GROUP * SPAN
BLOCK = 1024
PER = BLOCK // SPAN
PAIR = 2 * ROWS
CHUNK = 16
FACTOR = math.log2(math.e) / math.sqrt(D)
LOW = -1e30
META = 16
PIECE = 4 * SPAN + META
PAGE = GROUP * D + D
PACK = 2 * SPAN + META + 4 * SPAN
RANK, FULL, TURN, SLOT, HAVE = range(5)
NT = (((1,), (1,)), ((), ()))
VMEM_SPEC = pl.BlockSpec(memory_space=pltpu.VMEM)
SMEM_SPEC = pl.BlockSpec(memory_space=pltpu.SMEM)
ANY_SPEC = pl.BlockSpec(memory_space=pl.ANY)


SMALL = pltpu.CompilerParams(vmem_limit_bytes=8 * 2**20)
PARAMS = pltpu.CompilerParams(vmem_limit_bytes=24 * 2**20)


def shift(x, axis, by):
    size = 2 if axis == "c" else 4
    return lax.ppermute(x, axis, [(i, (i + by) % size) for i in range(size)])


def cross(x, axis, by):
    if axis == "z":
        axes, at = ("z", "c"), lambda i, c: 2 * i + c
    else:
        axes, at = ("xh", "c", "xl"), lambda i, c: i // 2 * 4 + c * 2 + i % 2
    pairs = [(at(i, c), at((i + by) % 4, 1 - c)) for i in range(4) for c in range(2)]
    return lax.ppermute(x, axes, pairs)


def prep_kernel(pos_ref, slot_ref, q_ref, k_ref, ks_ref, v_ref, vs_ref, out):
    rows = k_ref.shape[0]
    row = lax.broadcasted_iota(jnp.int32, (META, 2 * D), 0)
    meta = jnp.zeros((META, 2 * D), F32)
    for r in range(2):
        meta = jnp.where(row == r, pos_ref[r].astype(F32), meta)
        meta = jnp.where(row == 2 + r, slot_ref[r].astype(F32), meta)
    ks, vs = ks_ref[...].astype(F32).T, vs_ref[...].astype(F32).T
    for h in range(HEADS):
        at = slice(h * D, (h + 1) * D)
        out[h, :rows, :D] = (k_ref[:, at].astype(F32) * ks[:, h : h + 1]).astype(BF16)
        out[h, :rows, D:] = (v_ref[:, at].astype(F32) * vs[:, h : h + 1]).astype(BF16)
        out[h, rows : rows + META, :] = meta.astype(BF16)
        for i in range(2):
            first = rows + META + i * rows
            at = slice((h * 2 + i) * 2 * D, (h * 2 + i + 1) * 2 * D)
            out[h, first : first + rows, :] = q_ref[:, at]


def prep(pos, slot, queries, k, ks, v, vs):
    return pl.pallas_call(
        prep_kernel,
        out_shape=jax.ShapeDtypeStruct((HEADS, PACK, 2 * D), BF16),
        in_specs=[SMEM_SPEC] * 2 + [VMEM_SPEC] * 5,
        out_specs=VMEM_SPEC,
        name="prep",
    )(pos, slot, queries, k, ks.T, v, vs.T)


def split_kernel(x_ref, a_ref, b_ref, q_ref, note_ref):
    note = jnp.concatenate([x_ref[y, 2 * SPAN : 2 * SPAN + META, :].astype(F32)[:4] for y in range(4)], axis=0)
    note = note.astype(BF16)
    note_ref[...] = note
    for i, ref in enumerate((a_ref, b_ref)):
        for y in range(4):
            ref[y * SPAN : (y + 1) * SPAN, :] = x_ref[y, i * SPAN : (i + 1) * SPAN, :]
        ref[4 * SPAN :, :] = note
    rows = 2 * SPAN
    for y in range(4):
        for i in range(2):
            first = rows + META + i * rows
            q_ref[y * rows : (y + 1) * rows, i * 2 * D : (i + 1) * 2 * D] = x_ref[y, first : first + rows, :]


def split(x):
    return pl.pallas_call(
        split_kernel,
        out_shape=(
            jax.ShapeDtypeStruct((PIECE, 2 * D), BF16),
            jax.ShapeDtypeStruct((PIECE, 2 * D), BF16),
            jax.ShapeDtypeStruct((8 * SPAN, GROUP * D), BF16),
            jax.ShapeDtypeStruct((META, 2 * D), BF16),
        ),
        in_specs=[VMEM_SPEC],
        out_specs=(VMEM_SPEC,) * 4,
        compiler_params=SMALL,
        name="split",
    )(x)


def copy_kernel(moves, inputs, *refs):
    ins, rest = refs[:inputs], refs[inputs:]
    outs, sem = rest[:-1], rest[-1]
    copies = [
        pltpu.make_async_copy(ins[i].at[pl.ds(a, n), :], outs[o].at[pl.ds(b, n), :], sem.at[c])
        for c, (i, a, o, b, n) in enumerate(moves)
    ]
    for copy in copies:
        copy.start()
    for copy in copies:
        copy.wait()


def move(name, moves, rows, *arrays):
    return pl.pallas_call(
        functools.partial(copy_kernel, moves, len(arrays)),
        out_shape=tuple(jax.ShapeDtypeStruct((r, 2 * D), BF16) for r in rows),
        in_specs=[ANY_SPEC] * len(arrays),
        out_specs=(VMEM_SPEC,) * len(rows),
        scratch_shapes=[pltpu.SemaphoreType.DMA((len(moves),))],
        compiler_params=SMALL,
        name=name,
    )(*arrays)


def offsets(pieces):
    return [p * PIECE + y * SPAN for p in range(pieces) for y in range(4)]


def load_parts(parts, kv_s, sem):
    copies, row = [], 0
    for i, part in enumerate(parts):
        copies.append(pltpu.make_async_copy(part, kv_s.at[pl.ds(row, part.shape[0]), :], sem.at[i]))
        row += part.shape[0]
    for copy in copies:
        copy.start()
    return copies


def tables(kinds, kv_s, note_refs, tab_v, tab, sem, have=None):
    count = len(kinds) * 4
    row = lax.broadcasted_iota(jnp.int32, (META, D), 0)
    lane = lax.broadcasted_iota(jnp.int32, (META, D), 1)
    place = jnp.zeros((1, D), F32)
    for p, kind in enumerate(kinds):
        x = kv_s[p * PIECE + 4 * SPAN : (p + 1) * PIECE, :D].astype(F32)
        hit = jnp.logical_and(row == (lane - p * 4) * 4 + kind, jnp.logical_and(lane >= p * 4, lane < p * 4 + 4))
        place = place + jnp.sum(jnp.where(hit, x, 0.0), axis=0, keepdims=True)
    q_place, slot = jnp.zeros((1, D), F32), jnp.zeros((1, D), F32)
    for half, ref in enumerate(note_refs):
        x = ref[:, :D].astype(F32)
        j = lane - half * 8
        hit = jnp.logical_and(jnp.logical_and(j >= 0, j < 8), row == (j // 2) * 4 + j % 2)
        q_place = q_place + jnp.sum(jnp.where(hit, x, 0.0), axis=0, keepdims=True)
        hit = jnp.logical_and(jnp.logical_and(j >= 0, j < 8), row == (j // 2) * 4 + j % 2 + 2)
        slot = slot + jnp.sum(jnp.where(hit, x, 0.0), axis=0, keepdims=True)
    big_row = lax.broadcasted_iota(jnp.int32, (D, D), 0)
    down = jnp.broadcast_to(place, (D, D)).T
    inside = big_row < count

    def below(x, limit, where):
        return jnp.sum(jnp.where(jnp.logical_and(x < limit, where), 1.0, 0.0), axis=0, keepdims=True).astype(jnp.int32)

    tab_v[RANK : RANK + 1, :] = below(down, place, inside)
    tab_v[FULL : FULL + 1, :] = below(down, q_place, inside)
    q_down = jnp.broadcast_to(q_place, (D, D)).T
    big_lane = lax.broadcasted_iota(jnp.int32, (D, D), 1)
    same = jnp.logical_and(big_row // 8 == big_lane // 8, big_row < 8 * len(note_refs))
    tab_v[TURN : TURN + 1, :] = below(q_down, q_place, same) + lane[:1] // 8 * 8
    at = ((big_row // 4) * PIECE + big_row % 4 * SPAN + 1).astype(F32)
    hit = jnp.logical_and(down == slot, inside)
    tab_v[SLOT : SLOT + 1, :] = jnp.sum(jnp.where(hit, at, 0.0), axis=0, keepdims=True).astype(jnp.int32) - 1
    if have is not None:
        tab_v[HAVE : HAVE + 1, :] = have[...]
    copy = pltpu.make_async_copy(tab_v, tab, sem)
    copy.start()
    copy.wait()


def place_queries(q_refs, tab, q_s):
    for half, q_ref in enumerate(q_refs):
        for j in range(8):
            first = tab[TURN, half * 8 + j] * ROWS
            for g in range(GROUP):
                at = pl.ds(pl.multiple_of(first + g * SPAN, SPAN), SPAN)
                q_s[at, :] = q_ref[j * SPAN : (j + 1) * SPAN, g * D : (g + 1) * D]


def flash(spans, count, diagonal, tab, q_s, kv_s, m_s, acc, work):
    s_a, s_b, p_a, p_b, al_a, al_b, order, full_s, own_s, it_q, it_k, it_sub = work
    for i, row in enumerate(offsets(spans // 4)):
        order[tab[RANK, i]] = row
    for j in range(count):
        full_s[tab[TURN, j]] = tab[FULL, j] * SPAN
        own_s[tab[TURN, j]] = 1 if diagonal and j < 8 else 0

    total = jnp.int32(0)
    for pair in range(count // 2):
        keys = jnp.maximum(
            full_s[2 * pair] + own_s[2 * pair] * SPAN,
            full_s[2 * pair + 1] + own_s[2 * pair + 1] * SPAN,
        )
        blocks = (keys + BLOCK - 1) // BLOCK

        def put(b, _, pair=pair, total=total):
            it_q[total + b] = pair
            it_k[total + b] = b * PER
            it_sub[total + b] = b * BLOCK
            return 0

        lax.fori_loop(0, blocks, put, 0)
        total = total + blocks
    for extra in range(3):
        it_q[total + extra] = 0
        it_k[total + extra] = 0
        it_sub[total + extra] = 1 << 20

    def rows_of(t):
        return pl.ds(pl.multiple_of(it_q[t] * PAIR, PAIR), PAIR)

    def keys_of(t, lanes):
        first = it_k[t]
        return jnp.concatenate(
            [kv_s[pl.ds(pl.multiple_of(order[first + i], 16), SPAN), lanes] for i in range(PER)], axis=0
        )

    def scores(t, s):
        s[...] = lax.dot_general(
            q_s[rows_of(t), :], keys_of(t, slice(0, D)), NT, preferred_element_type=F32
        )

    def weigh(t, s, p, al):
        first = pl.multiple_of(it_q[t] * PAIR, PAIR)
        token = lax.broadcasted_iota(jnp.int32, (CHUNK, D), 0) + 1
        lane = lax.broadcasted_iota(jnp.int32, (CHUNK, D), 1)
        for c in range(PAIR // CHUNK):
            r = slice(c * CHUNK, (c + 1) * CHUNK)
            which = it_q[t] * 2 + c * CHUNK // ROWS
            limit = full_s[which] - it_sub[t]
            if diagonal:
                limit = limit + own_s[which] * (token + (c * CHUNK) % SPAN)
            tiles = []
            for u in range(BLOCK // D):
                x = s[r, u * D : (u + 1) * D]
                tiles.append(jnp.where(lane < limit - u * D, x, LOW))
            top = functools.reduce(jnp.maximum, tiles)
            top = jnp.broadcast_to(jnp.max(top, axis=1, keepdims=True), (CHUNK, D)) * FACTOR
            at = pl.ds(first + c * CHUNK, CHUNK)
            old = m_s[at, :]
            new = jnp.maximum(old, top)
            m_s[at, :] = new
            al[r, :] = jnp.exp2(old - new)
            for u in range(BLOCK // D):
                p[r, u * D : (u + 1) * D] = jnp.exp2(tiles[u] * FACTOR - new).astype(BF16)

    def gather(t, p, al_ref):
        v = keys_of(t, slice(D, 2 * D))
        v = jnp.concatenate([v, jnp.ones((BLOCK, D), BF16)], axis=1)
        o = lax.dot(p[...], v, preferred_element_type=F32)
        al = al_ref[...]
        rows = rows_of(t)
        acc[rows, :] = acc[rows, :] * jnp.concatenate([al, al], axis=1) + o

    scores(0, s_a)

    def body(i, _):
        t = 2 * i
        scores(t + 1, s_b)
        weigh(t, s_a, p_a, al_a)
        gather(t, p_a, al_a)
        scores(t + 2, s_a)
        weigh(t + 1, s_b, p_b, al_b)
        gather(t + 1, p_b, al_b)
        return 0

    lax.fori_loop(0, (total + 1) // 2, body, 0)


def work_shapes(spans, count):
    items = count // 2 * (spans // PER + 1) + 8
    return [
        pltpu.VMEM((PAIR, BLOCK), F32),
        pltpu.VMEM((PAIR, BLOCK), F32),
        pltpu.VMEM((PAIR, BLOCK), BF16),
        pltpu.VMEM((PAIR, BLOCK), BF16),
        pltpu.VMEM((PAIR, D), F32),
        pltpu.VMEM((PAIR, D), F32),
        pltpu.SMEM((spans + PER,), jnp.int32),
        pltpu.SMEM((count,), jnp.int32),
        pltpu.SMEM((count,), jnp.int32),
        pltpu.SMEM((items,), jnp.int32),
        pltpu.SMEM((items,), jnp.int32),
        pltpu.SMEM((items,), jnp.int32),
    ]


def scratch(spans, count, parts):
    return [
        pltpu.VMEM((spans // 4 * PIECE, 2 * D), BF16),
        pltpu.VMEM((count * ROWS, D), BF16),
        pltpu.SemaphoreType.DMA((parts,)),
        pltpu.VMEM((8, D), jnp.int32),
        pltpu.SMEM((8, D), jnp.int32),
        pltpu.SemaphoreType.DMA,
    ] + work_shapes(spans, count)


def chunk_row(tab, j):
    return pl.ds(pl.multiple_of(jnp.maximum(tab[SLOT, j], 0), 16), SPAN)


def first_kernel(na_ref, nb_ref, qa_ref, qb_ref, *refs):
    parts, (m_s, acc, page, have), rest = refs[:2], refs[2:6], refs[6:]
    kv_s, q_s, sem, tab_v, tab, tab_sem, *work = rest
    copies = load_parts(parts, kv_s, sem)
    m_s[...] = jnp.full(m_s.shape, LOW, F32)
    acc[...] = jnp.zeros(acc.shape, F32)
    for copy in copies:
        copy.wait()
    tables((0,) * 4 + (1,) * 4, kv_s, (na_ref, nb_ref), tab_v, tab, tab_sem)
    have[...] = tab_v[SLOT : SLOT + 1, :]
    for j in range(16):
        page[j] = kv_s[chunk_row(tab, j), :]
    place_queries((qa_ref, qb_ref), tab, q_s)
    flash(32, 16, True, tab, q_s, kv_s, m_s, acc, work)


def give_kernel(note_ref, q_ref, m_in, acc_in, page_in, *refs):
    parts, give, rest = refs[:4], refs[4], refs[5:]
    m_s, acc, kv_s, q_s, sem, tab_v, tab, tab_sem, *work = rest
    copies = load_parts(parts, kv_s, sem)
    m_s[...] = m_in[8 * ROWS :, :]
    acc[...] = acc_in[8 * ROWS :, :]
    for copy in copies:
        copy.wait()
    tables((0,) * 8 + (1,) * 8, kv_s, (note_ref,), tab_v, tab, tab_sem)
    place_queries((q_ref,), tab, q_s)
    flash(64, 8, False, tab, q_s, kv_s, m_s, acc, work)
    lane = lax.broadcasted_iota(jnp.int32, (SPAN, D), 1)
    for j in range(8):
        at = slice(j * SPAN, (j + 1) * SPAN)
        packed = jnp.zeros((SPAN, D), F32)
        for g in range(GROUP):
            rows = pl.ds(pl.multiple_of(tab[TURN, j] * ROWS + g * SPAN, SPAN), SPAN)
            give[at, g * D : (g + 1) * D] = acc[rows, :D]
            packed = jnp.where(lane == g, m_s[rows, :], packed)
            packed = jnp.where(lane == GROUP + g, acc[rows, D:], packed)
        give[at, GROUP * D : PAGE] = packed
        found = tab[SLOT, j] >= 0
        give[at, PAGE:] = jnp.where(found, kv_s[chunk_row(tab, j), :].astype(F32), page_in[8 + j].astype(F32))


def second_kernel(note_ref, q_ref, m_in, acc_in, page_in, have_in, *refs):
    parts, (m_s, acc, page, have), rest = refs[:4], refs[4:8], refs[8:]
    kv_s, q_s, sem, tab_v, tab, tab_sem, *work = rest
    copies = load_parts(parts, kv_s, sem)
    m_s[...] = m_in[: 8 * ROWS, :]
    acc[...] = acc_in[: 8 * ROWS, :]
    for copy in copies:
        copy.wait()
    tables((0,) * 8 + (1,) * 8, kv_s, (note_ref,), tab_v, tab, tab_sem)
    have[...] = jnp.maximum(have_in[...], tab_v[SLOT : SLOT + 1, :])
    for j in range(8):
        page[j] = jnp.where(tab[SLOT, j] >= 0, kv_s[chunk_row(tab, j), :].astype(F32), page_in[j].astype(F32)).astype(BF16)
    place_queries((q_ref,), tab, q_s)
    flash(64, 8, False, tab, q_s, kv_s, m_s, acc, work)


def third_kernel(note_ref, have, q_ref, m_in, acc_in, take, page, *refs):
    parts, out, rest = refs[:4], refs[4], refs[5:]
    m_s, acc, kv_s, q_s, sem, tab_v, tab, tab_sem, *work = rest
    copies = load_parts(parts, kv_s, sem)
    for copy in copies:
        copy.wait()
    tables(((0,) * 4 + (1,) * 4) * 2, kv_s, (note_ref,), tab_v, tab, tab_sem, have)
    place_queries((q_ref,), tab, q_s)
    for j in range(8):
        at = slice(j * SPAN, (j + 1) * SPAN)
        for g in range(GROUP):
            rows = pl.ds(pl.multiple_of(tab[TURN, j] * ROWS + g * SPAN, SPAN), SPAN)
            stat = GROUP * D + g
            m_b = jnp.broadcast_to(take[at, stat : stat + 1], (SPAN, D))
            l_b = jnp.broadcast_to(take[at, stat + GROUP : stat + GROUP + 1], (SPAN, D))
            m_a = m_in[rows, :]
            top = jnp.maximum(m_a, m_b)
            w_a, w_b = jnp.exp2(m_a - top), jnp.exp2(m_b - top)
            m_s[rows, :] = top
            acc[rows, :D] = acc_in[rows, :D] * w_a + take[at, g * D : (g + 1) * D] * w_b
            acc[rows, D:] = acc_in[rows, D:] * w_a + l_b * w_b

    for j in range(8):
        y, s = divmod(j, 2)
        far = jnp.where(tab[HAVE, j] >= 0, page[j].astype(F32), take[j * SPAN : (j + 1) * SPAN, PAGE:])
        near = kv_s[chunk_row(tab, j), :].astype(F32)
        out[y, 2 * SPAN :, s * 2 * D : (s + 1) * 2 * D] = jnp.where(tab[SLOT, j] >= 0, near, far).astype(BF16)

    flash(64, 8, False, tab, q_s, kv_s, m_s, acc, work)
    for j in range(8):
        y, ab = divmod(j, 2)
        for g in range(GROUP):
            rows = pl.ds(pl.multiple_of(tab[TURN, j] * ROWS + g * SPAN, SPAN), SPAN)
            out[y, ab * SPAN : (ab + 1) * SPAN, g * D : (g + 1) * D] = (
                acc[rows, :D] * (1.0 / acc[rows, D:])
            ).astype(BF16)


def finish_kernel(x_ref, o_ref, k_ref, v_ref):
    for h in range(HEADS):
        o_ref[:, h * GROUP * D : (h + 1) * GROUP * D] = x_ref[h, : 2 * SPAN, :]
        for s in range(2):
            at = 2 * s * D
            k_ref[s, :, h * D : (h + 1) * D] = x_ref[h, 2 * SPAN :, at : at + D]
            v_ref[s, :, h * D : (h + 1) * D] = x_ref[h, 2 * SPAN :, at + D : at + 2 * D]


def cost(scores):
    return pl.CostEstimate(flops=scores * 2048, bytes_accessed=2**20, transcendentals=0)


HAVE_SHAPE = jax.ShapeDtypeStruct((1, D), jnp.int32)


def state_shape(count):
    return [jax.ShapeDtypeStruct((count * ROWS, D), F32), jax.ShapeDtypeStruct((count * ROWS, 2 * D), F32)]


STATE = [pltpu.VMEM((8 * ROWS, D), F32), pltpu.VMEM((8 * ROWS, 2 * D), F32)]


def first(notes, q, q_other, parts):
    return pl.pallas_call(
        first_kernel,
        out_shape=(*state_shape(16), jax.ShapeDtypeStruct((16, SPAN, 2 * D), BF16), HAVE_SHAPE),
        in_specs=[VMEM_SPEC] * 4 + [ANY_SPEC] * 2,
        out_specs=(VMEM_SPEC,) * 4,
        scratch_shapes=scratch(32, 16, 2),
        compiler_params=PARAMS,
        cost_estimate=cost(16 * ROWS * 1024),
        name="first",
    )(*notes, q, q_other, *parts)


def give(note, q, m, acc, page, parts):
    return pl.pallas_call(
        give_kernel,
        out_shape=jax.ShapeDtypeStruct((8 * SPAN, PAGE + 2 * D), F32),
        in_specs=[VMEM_SPEC] * 5 + [ANY_SPEC] * 4,
        out_specs=VMEM_SPEC,
        scratch_shapes=STATE + scratch(64, 8, 4),
        compiler_params=PARAMS,
        cost_estimate=cost(8 * ROWS * 2048),
        name="give",
    )(note, q, m, acc, page, *parts)


def second(note, q, m, acc, page, have, parts):
    return pl.pallas_call(
        second_kernel,
        out_shape=(*state_shape(8), jax.ShapeDtypeStruct((8, SPAN, 2 * D), BF16), HAVE_SHAPE),
        in_specs=[VMEM_SPEC] * 6 + [ANY_SPEC] * 4,
        out_specs=(VMEM_SPEC,) * 4,
        scratch_shapes=scratch(64, 8, 4),
        compiler_params=PARAMS,
        cost_estimate=cost(8 * ROWS * 2048),
        name="second",
    )(note, q, m, acc, page, have, *parts)


def third(note, have, q, m, acc, take, page, parts):
    return pl.pallas_call(
        third_kernel,
        out_shape=jax.ShapeDtypeStruct((4, 3 * SPAN, GROUP * D), BF16),
        in_specs=[VMEM_SPEC] * 7 + [ANY_SPEC] * 4,
        out_specs=VMEM_SPEC,
        scratch_shapes=STATE + scratch(64, 8, 4),
        compiler_params=PARAMS,
        cost_estimate=cost(8 * ROWS * 2048),
        name="third",
    )(note, have, q, m, acc, take, page, *parts)


def finish(x):
    return pl.pallas_call(
        finish_kernel,
        out_shape=(
            jax.ShapeDtypeStruct((2 * SPAN, HEADS * GROUP * D), BF16),
            jax.ShapeDtypeStruct((2, SPAN, HEADS * D), BF16),
            jax.ShapeDtypeStruct((2, SPAN, HEADS * D), BF16),
        ),
        in_specs=[VMEM_SPEC],
        out_specs=(VMEM_SPEC,) * 3,
        compiler_params=SMALL,
        name="finish",
    )(x)


def local(queries, k, ks, v, vs, span_pos, page_of_slot):
    pack = prep(span_pos, page_of_slot, queries, k, ks, v, vs)
    pack = lax.all_to_all(pack.reshape(HEADS * PACK, 2 * D), "y", 0, 0, tiled=True)
    a, b, q, note = split(pack.reshape(4, PACK, 2 * D))
    q_other, note_other = shift(q, "c", 1), shift(note, "c", 1)
    notes = (note, note_other)

    a1, a2, a3 = shift(a, "z", -1), shift(a, "z", 2), shift(a, "z", 1)
    b1, b2, b3 = shift(b, X, -1), shift(b, X, 2), shift(b, X, 1)
    b3, q_other = lax.optimization_barrier((b3, q_other))
    moves = [(i, 0, i // 4, i % 4 * PIECE, PIECE) for i in range(8)]
    a, b = move("join", moves, (4 * PIECE, 4 * PIECE), a, a1, a2, a3, b, b1, b2, b3)
    a_next, a_prev = shift(a, X, -1), shift(a, X, 1)
    b_next, b_prev = shift(b, "z", -1), shift(b, "z", 1)

    m, acc, page, have = first(notes, q, q_other, (a, b))

    near = (a_next, a_prev, b_next, b_prev)
    near, m, acc, page, have = lax.optimization_barrier((near, m, acc, page, have))
    a_next, a_prev, b_next, b_prev = near
    far = (shift(a_prev, X, 1), shift(b_prev, "z", 1), cross(a_next, X, -1), cross(b_next, "z", -1))

    take = shift(give(note_other, q_other, m, acc, page, near), "c", 1)
    m, acc, page, have = second(note, q, m, acc, page, have, near)
    out = third(note, have, q, m, acc, take, page, far)
    out = lax.all_to_all(out.reshape(4 * 3 * SPAN, GROUP * D), "y", 0, 0, tiled=True)
    return finish(out.reshape(4, 3 * SPAN, GROUP * D))


def solution(mesh):
    fine = Mesh(mesh.devices.reshape(2, 4, 2, 4, 2), AXES)
    rows, flat = P(AXES, None), P(AXES)
    return jax.shard_map(
        local,
        mesh=fine,
        in_specs=(rows, rows, rows, rows, rows, flat, flat),
        out_specs=(rows, P(AXES, None, None), P(AXES, None, None)),
        check_vma=False,
    )
```

time: 779 us -> 127 us (0.16)
  the two profiles are of different devices: /device:TPU:1 before, /device:TPU:5 now
where the time goes in v1:
time: 127 us; the launch traced here: 126 us
  Pallas kernels  65.4 us (51%)
  blocking collectives  29.6 us (23%)
  starting transfers between devices  22.5 us (18%)
  waiting for transfers between devices  8.15 us (6%)
    ppermute x15, starting transfers between devices, shift(): return lax.ppermute(x, axis, [(i, (i + by) % size) for i in range(size)])  18.1 us
    pallas_call x1, Pallas kernels, first(): pl.pallas_call(first_kernel, out_shape=(*state_shape(16), jax.ShapeDtypeS...  16.5 us
    all_to_all x1, blocking collectives, local(): lax.all_to_all(pack.reshape(HEADS * PACK, 2 * D), 'y', 0, 0, tiled=True)  15.7 us
    pallas_call x1, Pallas kernels, third(): pl.pallas_call(third_kernel, out_shape=jax.ShapeDtypeStruct((4, 3 * SPAN,...  15.2 us
    pallas_call x1, Pallas kernels, give(): pl.pallas_call(give_kernel, out_shape=jax.ShapeDtypeStruct((8 * SPAN, PAG...  14.5 us
    pallas_call x1, Pallas kernels, second(): pl.pallas_call(second_kernel, out_shape=(*state_shape(8), jax.ShapeDtypeS...  14.4 us
    all_to_all x1, blocking collectives, local(): lax.all_to_all(out.reshape(4 * 3 * SPAN, GROUP * D), 'y', 0, 0, tiled=True)  13.9 us
    ppermute x15, waiting for transfers between devices, shift(): return lax.ppermute(x, axis, [(i, (i + by) % size) for i in range(size)])  8.14 us
  transfers between devices with their start and end apart: 17, of which 3 were waited for; matrix products, arithmetic and copies ran while one was open for 0% of the time, Pallas kernels for 26%

profile of v1, /device:TPU:5, one launch (start us, length us, event | category | flops | bytes accessed | tf_op | source)
XLA Modules:
  0.0 126.4 jit_solution(9146627021608990076)
XLA Ops:
  0.6 2.4 %prep.1 = bf16[4,400,256]{2,1,0:T(8,128)(2,1)} custom-call(s32[2]{0:T(128)} %pos_ref.1, s32[2]{0:T(128)} %slot_ref.1, bf16[128,2048]{1,0:T(8,128)(2,1)} %q_ref.1, bf16[128,512]{1,0:T(8,128)(2,1)} %k_ref.1, bf16[4,128]{1,0:T(4,128)(2,1)} %bitcast.2, bf16[128,512]{1,0:T(8,128)(2,1)} %v_ref.1, bf16[4,128]{1,0:T(4,128)(2,1)} %bitcast.3), custom_call_target="tpu_custom_call" | custom-call | tf_op jit(solution)/shard_map/prep/pallas_call | solution.py:76
  3.0 15.7 %all_to_all.12.x_ref = bf16[4,400,256]{2,1,0:T(8,128)(2,1)S(1)} all-to-all(bf16[4,400,256]{2,1,0:T(8,128)(2,1)} %prep.1), channel_id=1, replica_groups=mesh['xh'=2,'z'=4,'c'=2,'y'=4,'xl'=2] {'y'}, dimensions={0} | all-to-all | bytes 1638400 | tf_op jit(solution)/shard_map/all_to_all | solution.py:514
  18.7 2.2 %collective-permute-start.6 = (bf16[512,512]{1,0:T(8,128)(2,1)S(1)}, bf16[512,512]{1,0:T(8,128)(2,1)S(1)}, u32[]{:S(2)}, u32[]{:S(2)}) collective-permute-start(bf16[512,512]{1,0:T(8,128)(2,1)S(1)} %get-tuple-element.28.qa_ref.q_ref), channel_id=1, source_target_pairs={{0,8},{8,0},{1,9},{9,1},{2,10},{10,2},{3,11},{11,3},{4,12},{12,4},... | collective-permute-start | bytes 1572872 | tf_op jit(solution)/shard_map/ppermute | solution.py:44
  20.9 0.9 collective-permute-start.5
  21.8 3.8 %collective-permute-start = (bf16[272,256]{1,0:T(8,128)(2,1)S(1)}, bf16[272,256]{1,0:T(8,128)(2,1)S(1)}, u32[]{:S(2)}, u32[]{:S(2)}) collective-permute-start(bf16[272,256]{1,0:T(8,128)(2,1)S(1)} %get-tuple-element.29.refs_0_), channel_id=1, source_target_pairs={{0,48},{16,0},{32,16},{48,32},{1,49},{17,1},{33,17},{49,33},{2,50}... | collective-permute-start | bytes 417800 | tf_op jit(solution)/shard_map/ppermute | solution.py:44
  25.6 0.7 collective-permute-start.2
  26.3 0.5 collective-permute-start.3
  26.8 4.6 %collective-permute-done.refs_1_ = bf16[272,256]{1,0:T(8,128)(2,1)S(1)} collective-permute-done((bf16[272,256]{1,0:T(8,128)(2,1)S(1)}, bf16[272,256]{1,0:T(8,128)(2,1)S(1)}, u32[]{:S(2)}, u32[]{:S(2)}) %collective-permute-start) | collective-permute-done | bytes 139296 | tf_op jit(solution)/shard_map/ppermute | solution.py:44
  31.9 1.3 %collective-permute-start.11 = (bf16[16,256]{1,0:T(8,128)(2,1)S(1)}, bf16[16,256]{1,0:T(8,128)(2,1)S(1)}, u32[]{:S(2)}, u32[]{:S(2)}) collective-permute-start(bf16[16,256]{1,0:T(8,128)(2,1)S(1)} %get-tuple-element.27.na_ref.note_ref), channel_id=1, source_target_pairs={{0,8},{8,0},{1,9},{9,1},{2,10},{10,2},{3,11},{11,3},{4,12},{12,4},... | collective-permute-start | bytes 24584 | tf_op jit(solution)/shard_map/ppermute | solution.py:44
  33.3 1.8 %collective-permute-done.2.refs_3_ = bf16[272,256]{1,0:T(8,128)(2,1)S(1)} collective-permute-done((bf16[272,256]{1,0:T(8,128)(2,1)S(1)}, bf16[272,256]{1,0:T(8,128)(2,1)S(1)}, u32[]{:S(2)}, u32[]{:S(2)}) %collective-permute-start.2) | collective-permute-done | bytes 139296 | tf_op jit(solution)/shard_map/ppermute | solution.py:44
  35.1 1.7 %collective-permute-done.4.refs_6_ = bf16[272,256]{1,0:T(8,128)(2,1)S(1)} collective-permute-done((bf16[272,256]{1,0:T(8,128)(2,1)S(1)}, bf16[272,256]{1,0:T(8,128)(2,1)S(1)}, u32[]{:S(2)}, u32[]{:S(2)}) %collective-permute-start.4) | collective-permute-done | bytes 139296 | tf_op jit(solution)/shard_map/ppermute | solution.py:44
  36.8 1.5 %join.1 = (bf16[1088,256]{1,0:T(8,128)(2,1)S(1)}, bf16[1088,256]{1,0:T(8,128)(2,1)S(1)}) custom-call(bf16[272,256]{1,0:T(8,128)(2,1)S(1)} %get-tuple-element.29.refs_0_, bf16[272,256]{1,0:T(8,128)(2,1)S(1)} %collective-permute-done.refs_1_, bf16[272,256]{1,0:T(8,128)(2,1)S(1)} %collective-permute-done.1.refs_2_, ...), custom_call_target="tpu_custom_call" | custom-call | tf_op jit(solution)/shard_map/join/pallas_call | solution.py:130
  38.3 0.6 collective-permute-start.7
  38.9 0.9 collective-permute-start.8
  39.9 3.4 %collective-permute-start.9 = (bf16[1088,256]{1,0:T(8,128)(2,1)S(1)}, bf16[1088,256]{1,0:T(8,128)(2,1)S(1)}, u32[]{:S(2)}, u32[]{:S(2)}) collective-permute-start(bf16[1088,256]{1,0:T(8,128)(2,1)S(1)} %get-tuple-element.33.refs_1_), channel_id=1, source_target_pairs={{0,48},{16,0},{32,16},{48,32},{1,49},{17,1},{33,17},{49,33},{2,50}... | collective-permute-start | bytes 1671176 | tf_op jit(solution)/shard_map/ppermute | solution.py:44
  43.3 16.5 %first.1 = (f32[4096,128]{1,0:T(8,128)S(1)}, f32[4096,256]{1,0:T(8,128)S(1)}, bf16[16,64,256]{2,1,0:T(8,128)(2,1)S(1)}, s32[1,128]{1,0:T(1,128)S(1)}) custom-call(bf16[16,256]{1,0:T(8,128)(2,1)S(1)} %get-tuple-element.27.na_ref.note_ref, bf16[16,256]{1,0:T(8,128)(2,1)S(1)} %collective-permute-done.11.nb_ref.note_ref, ...), custom_call_target="tpu_custom_call" | custom-call | flops 8589934592 | bytes 1048576 | tf_op jit(solution)/shard_map/first/pallas_call | solution.py:446
  59.8 14.5 %give.1 = f32[512,896]{1,0:T(8,128)S(1)} custom-call(bf16[16,256]{1,0:T(8,128)(2,1)S(1)} %collective-permute-done.11.nb_ref.note_ref, bf16[512,512]{1,0:T(8,128)(2,1)S(1)} %collective-permute-done.6.qb_ref.q_ref, f32[4096,128]{1,0:T(8,128)S(1)} %get-tuple-element.39.m_in, f32[4096,256]{1,0:T(8,128)S(1)} %get-tuple-element.40.acc_in, ...), custom_call_target="tpu_custom_call" | custom-call | flops 8589934592 | bytes 1048576 | tf_op jit(solution)/shard_map/give/pallas_call | solution.py:459
  74.3 3.2 %collective-permute-start.12 = (f32[512,896]{1,0:T(8,128)S(1)}, f32[512,896]{1,0:T(8,128)S(1)}, u32[]{:S(2)}, u32[]{:S(2)}) collective-permute-start(f32[512,896]{1,0:T(8,128)S(1)} %give.1), channel_id=1, source_target_pairs={{0,8},{8,0},{1,9},{9,1},{2,10},{10,2},{3,11},{11,3},{4,12},{12,4},... | collective-permute-start | bytes 5505032 | tf_op jit(solution)/shard_map/ppermute | solution.py:44
  77.5 1.7 %collective-permute-start.15 = (bf16[1088,256]{1,0:T(8,128)(2,1)S(1)}, bf16[1088,256]{1,0:T(8,128)(2,1)S(1)}, u32[]{:S(2)}, u32[]{:S(2)}) collective-permute-start(bf16[1088,256]{1,0:T(8,128)(2,1)S(1)} %collective-permute-done.7.refs_0_), channel_id=1, source_target_pairs={{0,73},{8,65},{1,8},{9,0},{64,9},{72,1},{65,72},{73,64},{2,75},{10... | collective-permute-start | bytes 1671176 | tf_op jit(solution)/shard_map/ppermute | solution.py:53
  79.2 2.7 %collective-permute-start.16 = (bf16[1088,256]{1,0:T(8,128)(2,1)S(1)}, bf16[1088,256]{1,0:T(8,128)(2,1)S(1)}, u32[]{:S(2)}, u32[]{:S(2)}) collective-permute-start(bf16[1088,256]{1,0:T(8,128)(2,1)S(1)} %collective-permute-done.9.refs_2_), channel_id=1, source_target_pairs={{0,56},{8,48},{16,8},{24,0},{32,24},{40,16},{48,40},{56,32},{1,57}... | collective-permute-start | bytes 1671176 | tf_op jit(solution)/shard_map/ppermute | solution.py:53
  81.9 14.4 %second.1 = (f32[2048,128]{1,0:T(8,128)S(1)}, f32[2048,256]{1,0:T(8,128)S(1)}, bf16[8,64,256]{2,1,0:T(8,128)(2,1)S(1)}, s32[1,128]{1,0:T(1,128)S(1)}) custom-call(bf16[16,256]{1,0:T(8,128)(2,1)S(1)} %get-tuple-element.27.na_ref.note_ref, bf16[512,512]{1,0:T(8,128)(2,1)S(1)} %get-tuple-element.28.qa_ref.q_ref, f32[4096,128]{1,0:T(8,128)S(1)} %get-tuple-element.39.m_in, ...), custom_call_target="tpu_custom_call" | custom-call | flops 8589934592 | bytes 1048576 | tf_op jit(solution)/shard_map/second/pallas_call | solution.py:472
  96.4 15.2 %third.1 = bf16[4,192,512]{2,1,0:T(8,128)(2,1)S(1)} custom-call(bf16[16,256]{1,0:T(8,128)(2,1)S(1)} %get-tuple-element.27.na_ref.note_ref, s32[1,128]{1,0:T(1,128)S(1)} %get-tuple-element.47.have, bf16[512,512]{1,0:T(8,128)(2,1)S(1)} %get-tuple-element.28.qa_ref.q_ref, f32[2048,128]{1,0:T(8,128)S(1)} %get-tuple-element.48.m_in, ...), custom_call_target="tpu_custom_call" | custom-call | flops 8589934592 | bytes 1048576 | tf_op jit(solution)/shard_map/third/pallas_call | solution.py:485
  111.6 13.9 %all_to_all.13.x_ref = bf16[4,192,512]{2,1,0:T(8,128)(2,1)S(1)} all-to-all(bf16[4,192,512]{2,1,0:T(8,128)(2,1)S(1)} %third.1), channel_id=1, replica_groups=mesh['xh'=2,'z'=4,'c'=2,'y'=4,'xl'=2] {'y'}, dimensions={0} | all-to-all | bytes 1572864 | tf_op jit(solution)/shard_map/all_to_all | solution.py:537
  125.4 0.9 finish.1
  (20 shorter events, 0.6 us)
Async XLA Ops:
  18.7 13.2 %collective-permute-start.6 = (bf16[512,512]{1,0:T(8,128)(2,1)S(1)}, bf16[512,512]{1,0:T(8,128)(2,1)S(1)}, u32[]{:S(2)}, u32[]{:S(2)}) collective-permute-start(bf16[512,512]{1,0:T(8,128)(2,1)S(1)} %get-tuple-element.28.qa_ref.q_ref), channel_id=1, source_target_pairs={{0,8},{8,0},{1,9},{9,1},{2,10},{10,2},{3,11},{11,3},{4,12},{12,4},... | collective-permute-start | bytes 1572872 | tf_op jit(solution)/shard_map/ppermute | solution.py:44
  20.9 5.4 %collective-permute-start.5 = (bf16[272,256]{1,0:T(8,128)(2,1)S(1)}, bf16[272,256]{1,0:T(8,128)(2,1)S(1)}, u32[]{:S(2)}, u32[]{:S(2)}) collective-permute-start(bf16[272,256]{1,0:T(8,128)(2,1)S(1)} %get-tuple-element.30.refs_4_), channel_id=1, source_target_pairs={{0,1},{1,64},{64,65},{65,0},{2,3},{3,66},{66,67},{67,2},{4,5},{5,6... | collective-permute-start | bytes 417800 | tf_op jit(solution)/shard_map/ppermute | solution.py:44
  21.8 9.6 %collective-permute-start = (bf16[272,256]{1,0:T(8,128)(2,1)S(1)}, bf16[272,256]{1,0:T(8,128)(2,1)S(1)}, u32[]{:S(2)}, u32[]{:S(2)}) collective-permute-start(bf16[272,256]{1,0:T(8,128)(2,1)S(1)} %get-tuple-element.29.refs_0_), channel_id=1, source_target_pairs={{0,48},{16,0},{32,16},{48,32},{1,49},{17,1},{33,17},{49,33},{2,50}... | collective-permute-start | bytes 417800 | tf_op jit(solution)/shard_map/ppermute | solution.py:44
  25.6 7.7 %collective-permute-start.1 = (bf16[272,256]{1,0:T(8,128)(2,1)S(1)}, bf16[272,256]{1,0:T(8,128)(2,1)S(1)}, u32[]{:S(2)}, u32[]{:S(2)}) collective-permute-start(bf16[272,256]{1,0:T(8,128)(2,1)S(1)} %get-tuple-element.29.refs_0_), channel_id=1, source_target_pairs={{0,32},{16,48},{32,0},{48,16},{1,33},{17,49},{33,1},{49,17},{2,34}... | collective-permute-start | bytes 417800 | tf_op jit(solution)/shard_map/ppermute | solution.py:44
  25.6 9.5 %collective-permute-start.2 = (bf16[272,256]{1,0:T(8,128)(2,1)S(1)}, bf16[272,256]{1,0:T(8,128)(2,1)S(1)}, u32[]{:S(2)}, u32[]{:S(2)}) collective-permute-start(bf16[272,256]{1,0:T(8,128)(2,1)S(1)} %get-tuple-element.29.refs_0_), channel_id=1, source_target_pairs={{0,16},{16,32},{32,48},{48,0},{1,17},{17,33},{33,49},{49,1},{2,18}... | collective-permute-start | bytes 417800 | tf_op jit(solution)/shard_map/ppermute | solution.py:44
  26.3 8.8 %collective-permute-start.3 = (bf16[272,256]{1,0:T(8,128)(2,1)S(1)}, bf16[272,256]{1,0:T(8,128)(2,1)S(1)}, u32[]{:S(2)}, u32[]{:S(2)}) collective-permute-start(bf16[272,256]{1,0:T(8,128)(2,1)S(1)} %get-tuple-element.30.refs_4_), channel_id=1, source_target_pairs={{0,65},{1,0},{64,1},{65,64},{2,67},{3,2},{66,3},{67,66},{4,69},{5,... | collective-permute-start | bytes 417800 | tf_op jit(solution)/shard_map/ppermute | solution.py:44
  31.4 5.4 %collective-permute-start.4 = (bf16[272,256]{1,0:T(8,128)(2,1)S(1)}, bf16[272,256]{1,0:T(8,128)(2,1)S(1)}, u32[]{:S(2)}, u32[]{:S(2)}) collective-permute-start(bf16[272,256]{1,0:T(8,128)(2,1)S(1)} %get-tuple-element.30.refs_4_), channel_id=1, source_target_pairs={{0,64},{1,65},{64,0},{65,1},{2,66},{3,67},{66,2},{67,3},{4,68},{5,... | collective-permute-start | bytes 417800 | tf_op jit(solution)/shard_map/ppermute | solution.py:44
  31.9 11.3 %collective-permute-start.11 = (bf16[16,256]{1,0:T(8,128)(2,1)S(1)}, bf16[16,256]{1,0:T(8,128)(2,1)S(1)}, u32[]{:S(2)}, u32[]{:S(2)}) collective-permute-start(bf16[16,256]{1,0:T(8,128)(2,1)S(1)} %get-tuple-element.27.na_ref.note_ref), channel_id=1, source_target_pairs={{0,8},{8,0},{1,9},{9,1},{2,10},{10,2},{3,11},{11,3},{4,12},{12,4},... | collective-permute-start | bytes 24584 | tf_op jit(solution)/shard_map/ppermute | solution.py:44
  38.3 21.5 %collective-permute-start.7 = (bf16[1088,256]{1,0:T(8,128)(2,1)S(1)}, bf16[1088,256]{1,0:T(8,128)(2,1)S(1)}, u32[]{:S(2)}, u32[]{:S(2)}) collective-permute-start(bf16[1088,256]{1,0:T(8,128)(2,1)S(1)} %get-tuple-element.32.refs_0_), channel_id=1, source_target_pairs={{0,65},{1,0},{64,1},{65,64},{2,67},{3,2},{66,3},{67,66},{4,69},{5,... | collective-permute-start | bytes 1671176 | tf_op jit(solution)/shard_map/ppermute | solution.py:44
  38.9 20.9 %collective-permute-start.8 = (bf16[1088,256]{1,0:T(8,128)(2,1)S(1)}, bf16[1088,256]{1,0:T(8,128)(2,1)S(1)}, u32[]{:S(2)}, u32[]{:S(2)}) collective-permute-start(bf16[1088,256]{1,0:T(8,128)(2,1)S(1)} %get-tuple-element.32.refs_0_), channel_id=1, source_target_pairs={{0,1},{1,64},{64,65},{65,0},{2,3},{3,66},{66,67},{67,2},{4,5},{5,6... | collective-permute-start | bytes 1671176 | tf_op jit(solution)/shard_map/ppermute | solution.py:44
  39.9 20.0 %collective-permute-start.10 = (bf16[1088,256]{1,0:T(8,128)(2,1)S(1)}, bf16[1088,256]{1,0:T(8,128)(2,1)S(1)}, u32[]{:S(2)}, u32[]{:S(2)}) collective-permute-start(bf16[1088,256]{1,0:T(8,128)(2,1)S(1)} %get-tuple-element.33.refs_1_), channel_id=1, source_target_pairs={{0,16},{16,32},{32,48},{48,0},{1,17},{17,33},{33,49},{49,1},{2,18}... | collective-permute-start | bytes 1671176 | tf_op jit(solution)/shard_map/ppermute | solution.py:44
  39.9 20.0 %collective-permute-start.9 = (bf16[1088,256]{1,0:T(8,128)(2,1)S(1)}, bf16[1088,256]{1,0:T(8,128)(2,1)S(1)}, u32[]{:S(2)}, u32[]{:S(2)}) collective-permute-start(bf16[1088,256]{1,0:T(8,128)(2,1)S(1)} %get-tuple-element.33.refs_1_), channel_id=1, source_target_pairs={{0,48},{16,0},{32,16},{48,32},{1,49},{17,1},{33,17},{49,33},{2,50}... | collective-permute-start | bytes 1671176 | tf_op jit(solution)/shard_map/ppermute | solution.py:44
  74.3 22.1 %collective-permute-start.12 = (f32[512,896]{1,0:T(8,128)S(1)}, f32[512,896]{1,0:T(8,128)S(1)}, u32[]{:S(2)}, u32[]{:S(2)}) collective-permute-start(f32[512,896]{1,0:T(8,128)S(1)} %give.1), channel_id=1, source_target_pairs={{0,8},{8,0},{1,9},{9,1},{2,10},{10,2},{3,11},{11,3},{4,12},{12,4},... | collective-permute-start | bytes 5505032 | tf_op jit(solution)/shard_map/ppermute | solution.py:44
  77.5 18.9 %collective-permute-start.13 = (bf16[1088,256]{1,0:T(8,128)(2,1)S(1)}, bf16[1088,256]{1,0:T(8,128)(2,1)S(1)}, u32[]{:S(2)}, u32[]{:S(2)}) collective-permute-start(bf16[1088,256]{1,0:T(8,128)(2,1)S(1)} %collective-permute-done.8.refs_1_), channel_id=1, source_target_pairs={{0,1},{1,64},{64,65},{65,0},{2,3},{3,66},{66,67},{67,2},{4,5},{5,6... | collective-permute-start | bytes 1671176 | tf_op jit(solution)/shard_map/ppermute | solution.py:44
  77.5 18.9 %collective-permute-start.14 = (bf16[1088,256]{1,0:T(8,128)(2,1)S(1)}, bf16[1088,256]{1,0:T(8,128)(2,1)S(1)}, u32[]{:S(2)}, u32[]{:S(2)}) collective-permute-start(bf16[1088,256]{1,0:T(8,128)(2,1)S(1)} %collective-permute-done.10.refs_3_), channel_id=1, source_target_pairs={{0,16},{16,32},{32,48},{48,0},{1,17},{17,33},{33,49},{49,1},{2,18}... | collective-permute-start | bytes 1671176 | tf_op jit(solution)/shard_map/ppermute | solution.py:44
  77.5 18.9 %collective-permute-start.15 = (bf16[1088,256]{1,0:T(8,128)(2,1)S(1)}, bf16[1088,256]{1,0:T(8,128)(2,1)S(1)}, u32[]{:S(2)}, u32[]{:S(2)}) collective-permute-start(bf16[1088,256]{1,0:T(8,128)(2,1)S(1)} %collective-permute-done.7.refs_0_), channel_id=1, source_target_pairs={{0,73},{8,65},{1,8},{9,0},{64,9},{72,1},{65,72},{73,64},{2,75},{10... | collective-permute-start | bytes 1671176 | tf_op jit(solution)/shard_map/ppermute | solution.py:53
  79.2 17.2 %collective-permute-start.16 = (bf16[1088,256]{1,0:T(8,128)(2,1)S(1)}, bf16[1088,256]{1,0:T(8,128)(2,1)S(1)}, u32[]{:S(2)}, u32[]{:S(2)}) collective-permute-start(bf16[1088,256]{1,0:T(8,128)(2,1)S(1)} %collective-permute-done.9.refs_2_), channel_id=1, source_target_pairs={{0,56},{8,48},{16,8},{24,0},{32,24},{40,16},{48,40},{56,32},{1,57}... | collective-permute-start | bytes 1671176 | tf_op jit(solution)/shard_map/ppermute | solution.py:53

commit v2 on v1

--- a/solution.py
+++ b/solution.py
@@ -26,9 +26,8 @@
 LOW = -1e30
 META = 16
 PIECE = 4 * SPAN + META
-PAGE = GROUP * D + D
 PACK = 2 * SPAN + META + 4 * SPAN
-RANK, FULL, TURN, SLOT, HAVE = range(5)
+RANK, FULL, TURN, SLOT = range(4)
 NT = (((1,), (1,)), ((), ()))
 VMEM_SPEC = pl.BlockSpec(memory_space=pltpu.VMEM)
 SMEM_SPEC = pl.BlockSpec(memory_space=pltpu.SMEM)
@@ -152,7 +151,7 @@
     return copies
 
 
-def tables(kinds, kv_s, note_refs, tab_v, tab, sem, have=None):
+def tables(kinds, kv_s, note_refs, tab_v, tab, sem):
     count = len(kinds) * 4
     row = lax.broadcasted_iota(jnp.int32, (META, D), 0)
     lane = lax.broadcasted_iota(jnp.int32, (META, D), 1)
@@ -185,8 +184,6 @@
     at = ((big_row // 4) * PIECE + big_row % 4 * SPAN + 1).astype(F32)
     hit = jnp.logical_and(down == slot, inside)
     tab_v[SLOT : SLOT + 1, :] = jnp.sum(jnp.where(hit, at, 0.0), axis=0, keepdims=True).astype(jnp.int32) - 1
-    if have is not None:
-        tab_v[HAVE : HAVE + 1, :] = have[...]
     copy = pltpu.make_async_copy(tab_v, tab, sem)
     copy.start()
     copy.wait()
@@ -202,93 +199,110 @@
 
 
 def flash(spans, count, diagonal, tab, q_s, kv_s, m_s, acc, work):
-    s_a, s_b, p_a, p_b, al_a, al_b, order, full_s, own_s, it_q, it_k, it_sub = work
+    s_a, s_b, p_a, p_b, al_a, al_b, hot, order, full_s, own_s, wide, tail = work
     for i, row in enumerate(offsets(spans // 4)):
         order[tab[RANK, i]] = row
     for j in range(count):
-        full_s[tab[TURN, j]] = tab[FULL, j] * SPAN
+        full_s[tab[TURN, j]] = tab[FULL, j]
         own_s[tab[TURN, j]] = 1 if diagonal and j < 8 else 0
-
-    total = jnp.int32(0)
+    if not diagonal:
+        key = lax.broadcasted_iota(jnp.int32, (BLOCK, D), 0)
+        hot[...] = jnp.where(lax.broadcasted_iota(jnp.int32, (BLOCK, D), 1) == key // SPAN, 1.0, 0.0).astype(BF16)
+
+    n_wide, n_tail = jnp.int32(0), jnp.int32(0)
     for pair in range(count // 2):
-        keys = jnp.maximum(
-            full_s[2 * pair] + own_s[2 * pair] * SPAN,
-            full_s[2 * pair + 1] + own_s[2 * pair + 1] * SPAN,
-        )
-        blocks = (keys + BLOCK - 1) // BLOCK
-
-        def put(b, _, pair=pair, total=total):
-            it_q[total + b] = pair
-            it_k[total + b] = b * PER
-            it_sub[total + b] = b * BLOCK
+        seen = jnp.maximum(full_s[2 * pair] + own_s[2 * pair], full_s[2 * pair + 1] + own_s[2 * pair + 1])
+        rest = lax.rem(seen, PER)
+        blocks = lax.div(seen, PER) + (rest > PER // 2).astype(jnp.int32)
+
+        def put(b, _, pair=pair, n_wide=n_wide):
+            wide[0, n_wide + b] = pair
+            wide[1, n_wide + b] = b * PER
+            wide[2, n_wide + b] = b * PER
             return 0
 
         lax.fori_loop(0, blocks, put, 0)
-        total = total + blocks
-    for extra in range(3):
-        it_q[total + extra] = 0
-        it_k[total + extra] = 0
-        it_sub[total + extra] = 1 << 20
-
-    def rows_of(t):
-        return pl.ds(pl.multiple_of(it_q[t] * PAIR, PAIR), PAIR)
-
-    def keys_of(t, lanes):
-        first = it_k[t]
-        return jnp.concatenate(
-            [kv_s[pl.ds(pl.multiple_of(order[first + i], 16), SPAN), lanes] for i in range(PER)], axis=0
-        )
-
-    def scores(t, s):
-        s[...] = lax.dot_general(
-            q_s[rows_of(t), :], keys_of(t, slice(0, D)), NT, preferred_element_type=F32
-        )
-
-    def weigh(t, s, p, al):
-        first = pl.multiple_of(it_q[t] * PAIR, PAIR)
-        token = lax.broadcasted_iota(jnp.int32, (CHUNK, D), 0) + 1
-        lane = lax.broadcasted_iota(jnp.int32, (CHUNK, D), 1)
-        for c in range(PAIR // CHUNK):
-            r = slice(c * CHUNK, (c + 1) * CHUNK)
-            which = it_q[t] * 2 + c * CHUNK // ROWS
-            limit = full_s[which] - it_sub[t]
-            if diagonal:
-                limit = limit + own_s[which] * (token + (c * CHUNK) % SPAN)
-            tiles = []
-            for u in range(BLOCK // D):
-                x = s[r, u * D : (u + 1) * D]
-                tiles.append(jnp.where(lane < limit - u * D, x, LOW))
-            top = functools.reduce(jnp.maximum, tiles)
-            top = jnp.broadcast_to(jnp.max(top, axis=1, keepdims=True), (CHUNK, D)) * FACTOR
-            at = pl.ds(first + c * CHUNK, CHUNK)
-            old = m_s[at, :]
-            new = jnp.maximum(old, top)
-            m_s[at, :] = new
-            al[r, :] = jnp.exp2(old - new)
-            for u in range(BLOCK // D):
-                p[r, u * D : (u + 1) * D] = jnp.exp2(tiles[u] * FACTOR - new).astype(BF16)
-
-    def gather(t, p, al_ref):
-        v = keys_of(t, slice(D, 2 * D))
-        v = jnp.concatenate([v, jnp.ones((BLOCK, D), BF16)], axis=1)
-        o = lax.dot(p[...], v, preferred_element_type=F32)
-        al = al_ref[...]
-        rows = rows_of(t)
-        acc[rows, :] = acc[rows, :] * jnp.concatenate([al, al], axis=1) + o
-
-    scores(0, s_a)
-
-    def body(i, _):
-        t = 2 * i
-        scores(t + 1, s_b)
-        weigh(t, s_a, p_a, al_a)
-        gather(t, p_a, al_a)
-        scores(t + 2, s_a)
-        weigh(t + 1, s_b, p_b, al_b)
-        gather(t + 1, p_b, al_b)
-        return 0
-
-    lax.fori_loop(0, (total + 1) // 2, body, 0)
+        n_wide = n_wide + blocks
+        tail[0, n_tail] = pair
+        tail[1, n_tail] = jnp.minimum(blocks * PER, spans - PER // 2)
+        tail[2, n_tail] = blocks * PER
+        n_tail = n_tail + jnp.logical_and(rest > 0, rest <= PER // 2).astype(jnp.int32)
+    for items, n in ((wide, n_wide), (tail, n_tail)):
+        for extra in range(3):
+            items[0, n + extra] = 0
+            items[1, n + extra] = 0
+            items[2, n + extra] = 1 << 20
+
+    def sweep(size, items, total):
+        per, cols = size // SPAN, slice(0, size)
+
+        def rows_of(t):
+            return pl.ds(pl.multiple_of(items[0, t] * PAIR, PAIR), PAIR)
+
+        def keys_of(t, lanes):
+            first = items[1, t]
+            return jnp.concatenate(
+                [kv_s[pl.ds(pl.multiple_of(order[first + i], 16), SPAN), lanes] for i in range(per)], axis=0
+            )
+
+        def scores(t, s):
+            q, k = q_s[rows_of(t), :], keys_of(t, slice(0, D))
+            if not diagonal:
+                lane = lax.broadcasted_iota(jnp.int32, (ROWS, D), 1)
+                shut = [
+                    jnp.where(lane < full_s[items[0, t] * 2 + i] - items[2, t], 0.0, LOW).astype(BF16)
+                    for i in range(2)
+                ]
+                q = jnp.concatenate([q, jnp.concatenate(shut, axis=0)], axis=1)
+                k = jnp.concatenate([k, hot[cols, :]], axis=1)
+            s[:, cols] = lax.dot_general(q, k, NT, preferred_element_type=F32)
+
+        def weigh(t, s, p, al):
+            first = pl.multiple_of(items[0, t] * PAIR, PAIR)
+            token = lax.broadcasted_iota(jnp.int32, (CHUNK, D), 0) + 1
+            lane = lax.broadcasted_iota(jnp.int32, (CHUNK, D), 1)
+            for c in range(PAIR // CHUNK):
+                r = slice(c * CHUNK, (c + 1) * CHUNK)
+                tiles = [s[r, u * D : (u + 1) * D] for u in range(size // D)]
+                if diagonal:
+                    which = items[0, t] * 2 + c * CHUNK // ROWS
+                    limit = (full_s[which] - items[2, t]) * SPAN + own_s[which] * (token + (c * CHUNK) % SPAN)
+                    gap = lane - limit
+                    tiles = [jnp.where(gap < -u * D, x, LOW) for u, x in enumerate(tiles)]
+                top = functools.reduce(jnp.maximum, tiles)
+                top = jnp.broadcast_to(jnp.max(top, axis=1, keepdims=True), (CHUNK, D)) * FACTOR
+                at = pl.ds(first + c * CHUNK, CHUNK)
+                old = m_s[at, :]
+                new = jnp.maximum(old, top)
+                m_s[at, :] = new
+                al[r, :] = jnp.exp2(old - new)
+                for u, x in enumerate(tiles):
+                    p[r, u * D : (u + 1) * D] = jnp.exp2(x * FACTOR - new).astype(BF16)
+
+        def gather(t, p, al_ref):
+            v = keys_of(t, slice(D, 2 * D))
+            v = jnp.concatenate([v, jnp.ones((size, D), BF16)], axis=1)
+            o = lax.dot(p[:, cols], v, preferred_element_type=F32)
+            al = al_ref[...]
+            rows = rows_of(t)
+            acc[rows, :] = acc[rows, :] * jnp.concatenate([al, al], axis=1) + o
+
+        scores(0, s_a)
+
+        def body(i, _):
+            t = 2 * i
+            scores(t + 1, s_b)
+            weigh(t, s_a, p_a, al_a)
+            gather(t, p_a, al_a)
+            scores(t + 2, s_a)
+            weigh(t + 1, s_b, p_b, al_b)
+            gather(t + 1, p_b, al_b)
+            return 0
+
+        lax.fori_loop(0, (total + 1) // 2, body, 0)
+
+    sweep(BLOCK, wide, n_wide)
+    sweep(BLOCK // 2, tail, n_tail)
 
 
 def work_shapes(spans, count):
@@ -300,12 +314,12 @@
         pltpu.VMEM((PAIR, BLOCK), BF16),
         pltpu.VMEM((PAIR, D), F32),
         pltpu.VMEM((PAIR, D), F32),
+        pltpu.VMEM((BLOCK, D), BF16),
         pltpu.SMEM((spans + PER,), jnp.int32),
         pltpu.SMEM((count,), jnp.int32),
         pltpu.SMEM((count,), jnp.int32),
-        pltpu.SMEM((items,), jnp.int32),
-        pltpu.SMEM((items,), jnp.int32),
-        pltpu.SMEM((items,), jnp.int32),
+        pltpu.SMEM((3, items), jnp.int32),
+        pltpu.SMEM((3, count // 2 + 8), jnp.int32),
     ]
 
 
@@ -341,82 +355,79 @@
 
 
 def give_kernel(note_ref, q_ref, m_in, acc_in, page_in, *refs):
-    parts, give, rest = refs[:4], refs[4], refs[5:]
-    m_s, acc, kv_s, q_s, sem, tab_v, tab, tab_sem, *work = rest
+    parts, (give_o, give_p), rest = refs[:4], refs[4:6], refs[6:]
+    m_s, acc, levels_s, kv_s, q_s, sem, tab_v, tab, tab_sem, *work = rest
     copies = load_parts(parts, kv_s, sem)
+    levels_s[...] = jnp.zeros(levels_s.shape, F32)
     m_s[...] = m_in[8 * ROWS :, :]
     acc[...] = acc_in[8 * ROWS :, :]
     for copy in copies:
         copy.wait()
     tables((0,) * 8 + (1,) * 8, kv_s, (note_ref,), tab_v, tab, tab_sem)
+    for j in range(8):
+        near = kv_s[chunk_row(tab, j), :].astype(F32)
+        give_p[j] = jnp.where(tab[SLOT, j] >= 0, near, page_in[8 + j].astype(F32)).astype(BF16)
     place_queries((q_ref,), tab, q_s)
     flash(64, 8, False, tab, q_s, kv_s, m_s, acc, work)
-    lane = lax.broadcasted_iota(jnp.int32, (SPAN, D), 1)
-    for j in range(8):
-        at = slice(j * SPAN, (j + 1) * SPAN)
-        packed = jnp.zeros((SPAN, D), F32)
-        for g in range(GROUP):
-            rows = pl.ds(pl.multiple_of(tab[TURN, j] * ROWS + g * SPAN, SPAN), SPAN)
-            give[at, g * D : (g + 1) * D] = acc[rows, :D]
-            packed = jnp.where(lane == g, m_s[rows, :], packed)
-            packed = jnp.where(lane == GROUP + g, acc[rows, D:], packed)
-        give[at, GROUP * D : PAGE] = packed
-        found = tab[SLOT, j] >= 0
-        give[at, PAGE:] = jnp.where(found, kv_s[chunk_row(tab, j), :].astype(F32), page_in[8 + j].astype(F32))
-
-
-def second_kernel(note_ref, q_ref, m_in, acc_in, page_in, have_in, *refs):
-    parts, (m_s, acc, page, have), rest = refs[:4], refs[4:8], refs[8:]
-    kv_s, q_s, sem, tab_v, tab, tab_sem, *work = rest
+    for g in range(GROUP):
+        for block in range(4):
+            logs = []
+            for j in (2 * block, 2 * block + 1):
+                rows = pl.ds(pl.multiple_of(tab[TURN, j] * ROWS + g * SPAN, SPAN), SPAN)
+                sums = jnp.maximum(acc[rows, D:], 1e-30)
+                give_o[j * SPAN : (j + 1) * SPAN, g * D : (g + 1) * D] = (acc[rows, :D] * (1.0 / sums)).astype(BF16)
+                logs.append(m_s[rows, :] + jnp.log(sums) * math.log2(math.e))
+            level = jnp.concatenate(logs, axis=0).T[:1, :]
+            for part in range(3):
+                piece = level.astype(BF16).astype(F32)
+                level = level - piece
+                levels_s[part * 4 + g : part * 4 + g + 1, block * D : (block + 1) * D] = piece
+    give_o[8 * SPAN :, :] = levels_s[...].astype(BF16)
+
+
+def own_kernel(note_ref, q_ref, m_in, acc_in, page_in, have, *refs):
+    parts, (m_out, acc_out, page, found), rest = refs[:8], refs[8:12], refs[12:]
+    m_s, acc, kv_s, q_s, sem, tab_v, tab, tab_sem, *work = rest
     copies = load_parts(parts, kv_s, sem)
     m_s[...] = m_in[: 8 * ROWS, :]
     acc[...] = acc_in[: 8 * ROWS, :]
     for copy in copies:
         copy.wait()
-    tables((0,) * 8 + (1,) * 8, kv_s, (note_ref,), tab_v, tab, tab_sem)
-    have[...] = jnp.maximum(have_in[...], tab_v[SLOT : SLOT + 1, :])
+    tables((0,) * 8 + (1,) * 8 + ((0,) * 4 + (1,) * 4) * 2, kv_s, (note_ref,), tab_v, tab, tab_sem)
+    found[...] = jnp.maximum(have[...], tab_v[SLOT : SLOT + 1, :])
     for j in range(8):
-        page[j] = jnp.where(tab[SLOT, j] >= 0, kv_s[chunk_row(tab, j), :].astype(F32), page_in[j].astype(F32)).astype(BF16)
+        near = kv_s[chunk_row(tab, j), :].astype(F32)
+        page[j] = jnp.where(tab[SLOT, j] >= 0, near, page_in[j].astype(F32)).astype(BF16)
     place_queries((q_ref,), tab, q_s)
-    flash(64, 8, False, tab, q_s, kv_s, m_s, acc, work)
-
-
-def third_kernel(note_ref, have, q_ref, m_in, acc_in, take, page, *refs):
-    parts, out, rest = refs[:4], refs[4], refs[5:]
-    m_s, acc, kv_s, q_s, sem, tab_v, tab, tab_sem, *work = rest
-    copies = load_parts(parts, kv_s, sem)
-    for copy in copies:
-        copy.wait()
-    tables(((0,) * 4 + (1,) * 4) * 2, kv_s, (note_ref,), tab_v, tab, tab_sem, have)
-    place_queries((q_ref,), tab, q_s)
+    flash(128, 8, False, tab, q_s, kv_s, m_s, acc, work)
     for j in range(8):
-        at = slice(j * SPAN, (j + 1) * SPAN)
-        for g in range(GROUP):
-            rows = pl.ds(pl.multiple_of(tab[TURN, j] * ROWS + g * SPAN, SPAN), SPAN)
-            stat = GROUP * D + g
-            m_b = jnp.broadcast_to(take[at, stat : stat + 1], (SPAN, D))
-            l_b = jnp.broadcast_to(take[at, stat + GROUP : stat + GROUP + 1], (SPAN, D))
-            m_a = m_in[rows, :]
-            top = jnp.maximum(m_a, m_b)
-            w_a, w_b = jnp.exp2(m_a - top), jnp.exp2(m_b - top)
-            m_s[rows, :] = top
-            acc[rows, :D] = acc_in[rows, :D] * w_a + take[at, g * D : (g + 1) * D] * w_b
-            acc[rows, D:] = acc_in[rows, D:] * w_a + l_b * w_b
-
+        rows = pl.ds(pl.multiple_of(tab[TURN, j] * ROWS, ROWS), ROWS)
+        m_out[j * ROWS : (j + 1) * ROWS, :] = m_s[rows, :]
+        acc_out[j * ROWS : (j + 1) * ROWS, :] = acc[rows, :]
+
+
+def merge_kernel(m_in, acc_in, take, page, found, take_p, out):
+    levels = take[8 * SPAN :, :].astype(F32)
+    for g in range(GROUP):
+        level = levels[g : g + 1] + levels[4 + g : 5 + g] + levels[8 + g : 9 + g]
+        for block in range(4):
+            both = jnp.broadcast_to(level[:, block * D : (block + 1) * D], (D, D)).T
+            for j in (2 * block, 2 * block + 1):
+                y, ab = divmod(j, 2)
+                rows = slice(j * ROWS + g * SPAN, j * ROWS + (g + 1) * SPAN)
+                m_a, m_b = m_in[rows, :], both[j % 2 * SPAN : (j % 2 + 1) * SPAN]
+                top = jnp.maximum(m_a, m_b)
+                w_a, w_b = jnp.exp2(m_a - top), jnp.exp2(m_b - top)
+                o_b = take[j * SPAN : (j + 1) * SPAN, g * D : (g + 1) * D].astype(F32)
+                total = acc_in[rows, D:] * w_a + w_b
+                o = (acc_in[rows, :D] * w_a + o_b * w_b) * (1.0 / total)
+                out[y, ab * SPAN : (ab + 1) * SPAN, g * D : (g + 1) * D] = o.astype(BF16)
+    lane = lax.broadcasted_iota(jnp.int32, (1, D), 1)
     for j in range(8):
         y, s = divmod(j, 2)
-        far = jnp.where(tab[HAVE, j] >= 0, page[j].astype(F32), take[j * SPAN : (j + 1) * SPAN, PAGE:])
-        near = kv_s[chunk_row(tab, j), :].astype(F32)
-        out[y, 2 * SPAN :, s * 2 * D : (s + 1) * 2 * D] = jnp.where(tab[SLOT, j] >= 0, near, far).astype(BF16)
-
-    flash(64, 8, False, tab, q_s, kv_s, m_s, acc, work)
-    for j in range(8):
-        y, ab = divmod(j, 2)
-        for g in range(GROUP):
-            rows = pl.ds(pl.multiple_of(tab[TURN, j] * ROWS + g * SPAN, SPAN), SPAN)
-            out[y, ab * SPAN : (ab + 1) * SPAN, g * D : (g + 1) * D] = (
-                acc[rows, :D] * (1.0 / acc[rows, D:])
-            ).astype(BF16)
+        here = jnp.max(jnp.where(lane == j, found[...], -1), axis=1, keepdims=True) >= 0
+        x = jnp.where(here, page[j].astype(F32), take_p[j].astype(F32))
+        out[y, 2 * SPAN :, s * 2 * D : (s + 1) * 2 * D] = x.astype(BF16)
 
 
 def finish_kernel(x_ref, o_ref, k_ref, v_ref):
@@ -455,43 +466,44 @@
     )(*notes, q, q_other, *parts)
 
 
+PAGES = jax.ShapeDtypeStruct((8, SPAN, 2 * D), BF16)
+
+
 def give(note, q, m, acc, page, parts):
     return pl.pallas_call(
         give_kernel,
-        out_shape=jax.ShapeDtypeStruct((8 * SPAN, PAGE + 2 * D), F32),
+        out_shape=(jax.ShapeDtypeStruct((8 * SPAN + META, GROUP * D), BF16), PAGES),
         in_specs=[VMEM_SPEC] * 5 + [ANY_SPEC] * 4,
-        out_specs=VMEM_SPEC,
-        scratch_shapes=STATE + scratch(64, 8, 4),
+        out_specs=(VMEM_SPEC,) * 2,
+        scratch_shapes=STATE + [pltpu.VMEM((META, GROUP * D), F32)] + scratch(64, 8, 4),
         compiler_params=PARAMS,
         cost_estimate=cost(8 * ROWS * 2048),
         name="give",
     )(note, q, m, acc, page, *parts)
 
 
-def second(note, q, m, acc, page, have, parts):
-    return pl.pallas_call(
-        second_kernel,
-        out_shape=(*state_shape(8), jax.ShapeDtypeStruct((8, SPAN, 2 * D), BF16), HAVE_SHAPE),
-        in_specs=[VMEM_SPEC] * 6 + [ANY_SPEC] * 4,
+def own(note, q, m, acc, page, have, parts):
+    return pl.pallas_call(
+        own_kernel,
+        out_shape=(*state_shape(8), PAGES, HAVE_SHAPE),
+        in_specs=[VMEM_SPEC] * 6 + [ANY_SPEC] * 8,
         out_specs=(VMEM_SPEC,) * 4,
-        scratch_shapes=scratch(64, 8, 4),
+        scratch_shapes=STATE + scratch(128, 8, 8),
         compiler_params=PARAMS,
-        cost_estimate=cost(8 * ROWS * 2048),
-        name="second",
+        cost_estimate=cost(8 * ROWS * 4096),
+        name="own",
     )(note, q, m, acc, page, have, *parts)
 
 
-def third(note, have, q, m, acc, take, page, parts):
-    return pl.pallas_call(
-        third_kernel,
+def merge(m, acc, take, page, found, take_page):
+    return pl.pallas_call(
+        merge_kernel,
         out_shape=jax.ShapeDtypeStruct((4, 3 * SPAN, GROUP * D), BF16),
-        in_specs=[VMEM_SPEC] * 7 + [ANY_SPEC] * 4,
+        in_specs=[VMEM_SPEC] * 6,
         out_specs=VMEM_SPEC,
-        scratch_shapes=STATE + scratch(64, 8, 4),
-        compiler_params=PARAMS,
-        cost_estimate=cost(8 * ROWS * 2048),
-        name="third",
-    )(note, have, q, m, acc, take, page, *parts)
+        compiler_params=SMALL,
+        name="merge",
+    )(m, acc, take, page, found, take_page)
 
 
 def finish(x):
@@ -531,9 +543,10 @@
     a_next, a_prev, b_next, b_prev = near
     far = (shift(a_prev, X, 1), shift(b_prev, "z", 1), cross(a_next, X, -1), cross(b_next, "z", -1))
 
-    take = shift(give(note_other, q_other, m, acc, page, near), "c", 1)
-    m, acc, page, have = second(note, q, m, acc, page, have, near)
-    out = third(note, have, q, m, acc, take, page, far)
+    give_o, give_p = give(note_other, q_other, m, acc, page, near)
+    take, take_page = shift(give_o, "c", 1), shift(give_p, "c", 1)
+    m, acc, page, found = own(note, q, m, acc, page, have, (*near, *far))
+    out = merge(m, acc, take, page, found, take_page)
     out = lax.all_to_all(out.reshape(4 * 3 * SPAN, GROUP * D), "y", 0, 0, tiled=True)
     return finish(out.reshape(4, 3 * SPAN, GROUP * D))
 

time: 127 us -> 119 us (0.937)
  the two profiles are of different devices: /device:TPU:5 before, /device:TPU:37 now
where the time goes in v2:
time: 119 us; the launch traced here: 117 us
  Pallas kernels  56.8 us (48%)
  blocking collectives  28.4 us (24%)
  starting transfers between devices  27.9 us (23%)
  waiting for transfers between devices  3.23 us (3%)
    ppermute x16, starting transfers between devices, shift(): return lax.ppermute(x, axis, [(i, (i + by) % size) for i in range(size)])  25.5 us
    pallas_call x1, Pallas kernels, own(): pl.pallas_call(own_kernel, out_shape=(*state_shape(8), PAGES, HAVE_SHAPE)...  24.4 us
    all_to_all x1, blocking collectives, local(): lax.all_to_all(pack.reshape(HEADS * PACK, 2 * D), 'y', 0, 0, tiled=True)  15.7 us
    pallas_call x1, Pallas kernels, first(): pl.pallas_call(first_kernel, out_shape=(*state_shape(16), jax.ShapeDtypeS...  14.5 us
    all_to_all x1, blocking collectives, local(): lax.all_to_all(out.reshape(4 * 3 * SPAN, GROUP * D), 'y', 0, 0, tiled=True)  12.7 us
    pallas_call x1, Pallas kernels, give(): pl.pallas_call(give_kernel, out_shape=(jax.ShapeDtypeStruct((8 * SPAN + M...  12.4 us
  transfers between devices with their start and end apart: 18, of which 3 were waited for; matrix products, arithmetic and copies ran while one was open for 0% of the time, Pallas kernels for 45%

profile of v2, /device:TPU:37, one launch (start us, length us, event | category | flops | bytes accessed | tf_op | source)
XLA Modules:
  0.0 117.0 jit_solution(11615194065352929803)
XLA Ops:
  0.6 2.3 %prep.1 = bf16[4,400,256]{2,1,0:T(8,128)(2,1)} custom-call(s32[2]{0:T(128)} %pos_ref.1, s32[2]{0:T(128)} %slot_ref.1, bf16[128,2048]{1,0:T(8,128)(2,1)} %q_ref.1, bf16[128,512]{1,0:T(8,128)(2,1)} %k_ref.1, bf16[4,128]{1,0:T(4,128)(2,1)} %bitcast.2, bf16[128,512]{1,0:T(8,128)(2,1)} %v_ref.1, bf16[4,128]{1,0:T(4,128)(2,1)} %bitcast.3), custom_call_target="tpu_custom_call" | custom-call | tf_op jit(solution)/shard_map/prep/pallas_call | solution.py:75
  3.0 15.7 %all_to_all.12.x_ref = bf16[4,400,256]{2,1,0:T(8,128)(2,1)S(1)} all-to-all(bf16[4,400,256]{2,1,0:T(8,128)(2,1)} %prep.1), channel_id=1, replica_groups=mesh['xh'=2,'z'=4,'c'=2,'y'=4,'xl'=2] {'y'}, dimensions={0} | all-to-all | bytes 1638400 | tf_op jit(solution)/shard_map/all_to_all | solution.py:526
  18.7 2.2 %collective-permute-start.6 = (bf16[512,512]{1,0:T(8,128)(2,1)S(1)}, bf16[512,512]{1,0:T(8,128)(2,1)S(1)}, u32[]{:S(2)}, u32[]{:S(2)}) collective-permute-start(bf16[512,512]{1,0:T(8,128)(2,1)S(1)} %get-tuple-element.30.qa_ref.q_ref), channel_id=1, source_target_pairs={{0,8},{8,0},{1,9},{9,1},{2,10},{10,2},{3,11},{11,3},{4,12},{12,4},... | collective-permute-start | bytes 1572872 | tf_op jit(solution)/shard_map/ppermute | solution.py:43
  20.9 0.9 collective-permute-start.5
  21.8 2.8 %collective-permute-start.1 = (bf16[272,256]{1,0:T(8,128)(2,1)S(1)}, bf16[272,256]{1,0:T(8,128)(2,1)S(1)}, u32[]{:S(2)}, u32[]{:S(2)}) collective-permute-start(bf16[272,256]{1,0:T(8,128)(2,1)S(1)} %get-tuple-element.31.refs_0_), channel_id=1, source_target_pairs={{0,32},{16,48},{32,0},{48,16},{1,33},{17,49},{33,1},{49,17},{2,34}... | collective-permute-start | bytes 417800 | tf_op jit(solution)/shard_map/ppermute | solution.py:43
  24.6 1.9 %collective-permute-start.2 = (bf16[272,256]{1,0:T(8,128)(2,1)S(1)}, bf16[272,256]{1,0:T(8,128)(2,1)S(1)}, u32[]{:S(2)}, u32[]{:S(2)}) collective-permute-start(bf16[272,256]{1,0:T(8,128)(2,1)S(1)} %get-tuple-element.31.refs_0_), channel_id=1, source_target_pairs={{0,16},{16,32},{32,48},{48,0},{1,17},{17,33},{33,49},{49,1},{2,18}... | collective-permute-start | bytes 417800 | tf_op jit(solution)/shard_map/ppermute | solution.py:43
  27.1 2.0 %collective-permute-start.4 = (bf16[272,256]{1,0:T(8,128)(2,1)S(1)}, bf16[272,256]{1,0:T(8,128)(2,1)S(1)}, u32[]{:S(2)}, u32[]{:S(2)}) collective-permute-start(bf16[272,256]{1,0:T(8,128)(2,1)S(1)} %get-tuple-element.32.refs_4_), channel_id=1, source_target_pairs={{0,64},{1,65},{64,0},{65,1},{2,66},{3,67},{66,2},{67,3},{4,68},{5,... | collective-permute-start | bytes 417800 | tf_op jit(solution)/shard_map/ppermute | solution.py:43
  29.2 1.2 %collective-permute-start.11 = (bf16[16,256]{1,0:T(8,128)(2,1)S(1)}, bf16[16,256]{1,0:T(8,128)(2,1)S(1)}, u32[]{:S(2)}, u32[]{:S(2)}) collective-permute-start(bf16[16,256]{1,0:T(8,128)(2,1)S(1)} %get-tuple-element.29.na_ref.note_ref), channel_id=1, source_target_pairs={{0,8},{8,0},{1,9},{9,1},{2,10},{10,2},{3,11},{11,3},{4,12},{12,4},... | collective-permute-start | bytes 24584 | tf_op jit(solution)/shard_map/ppermute | solution.py:43
  30.5 1.4 %collective-permute-done.2.refs_3_ = bf16[272,256]{1,0:T(8,128)(2,1)S(1)} collective-permute-done((bf16[272,256]{1,0:T(8,128)(2,1)S(1)}, bf16[272,256]{1,0:T(8,128)(2,1)S(1)}, u32[]{:S(2)}, u32[]{:S(2)}) %collective-permute-start.2) | collective-permute-done | bytes 139296 | tf_op jit(solution)/shard_map/ppermute | solution.py:43
  31.8 0.7 collective-permute-done.4.refs_6_
  32.6 1.5 %join.1 = (bf16[1088,256]{1,0:T(8,128)(2,1)S(1)}, bf16[1088,256]{1,0:T(8,128)(2,1)S(1)}) custom-call(bf16[272,256]{1,0:T(8,128)(2,1)S(1)} %get-tuple-element.31.refs_0_, bf16[272,256]{1,0:T(8,128)(2,1)S(1)} %collective-permute-done.refs_1_, bf16[272,256]{1,0:T(8,128)(2,1)S(1)} %collective-permute-done.1.refs_2_, ...), custom_call_target="tpu_custom_call" | custom-call | tf_op jit(solution)/shard_map/join/pallas_call | solution.py:129
  34.1 2.0 %collective-permute-start.7 = (bf16[1088,256]{1,0:T(8,128)(2,1)S(1)}, bf16[1088,256]{1,0:T(8,128)(2,1)S(1)}, u32[]{:S(2)}, u32[]{:S(2)}) collective-permute-start(bf16[1088,256]{1,0:T(8,128)(2,1)S(1)} %get-tuple-element.34.refs_0_), channel_id=1, source_target_pairs={{0,65},{1,0},{64,1},{65,64},{2,67},{3,2},{66,3},{67,66},{4,69},{5,... | collective-permute-start | bytes 1671176 | tf_op jit(solution)/shard_map/ppermute | solution.py:43
  36.0 0.9 collective-permute-start.8
  36.9 5.0 %collective-permute-start.9 = (bf16[1088,256]{1,0:T(8,128)(2,1)S(1)}, bf16[1088,256]{1,0:T(8,128)(2,1)S(1)}, u32[]{:S(2)}, u32[]{:S(2)}) collective-permute-start(bf16[1088,256]{1,0:T(8,128)(2,1)S(1)} %get-tuple-element.35.refs_1_), channel_id=1, source_target_pairs={{0,48},{16,0},{32,16},{48,32},{1,49},{17,1},{33,17},{49,33},{2,50}... | collective-permute-start | bytes 1671176 | tf_op jit(solution)/shard_map/ppermute | solution.py:43
  41.9 14.5 %first.1 = (f32[4096,128]{1,0:T(8,128)S(1)}, f32[4096,256]{1,0:T(8,128)S(1)}, bf16[16,64,256]{2,1,0:T(8,128)(2,1)S(1)}, s32[1,128]{1,0:T(1,128)S(1)}) custom-call(bf16[16,256]{1,0:T(8,128)(2,1)S(1)} %get-tuple-element.29.na_ref.note_ref, bf16[16,256]{1,0:T(8,128)(2,1)S(1)} %collective-permute-done.11.nb_ref.note_ref, ...), custom_call_target="tpu_custom_call" | custom-call | flops 8589934592 | bytes 1048576 | tf_op jit(solution)/shard_map/first/pallas_call | solution.py:457
  56.5 1.9 %collective-permute-start.12 = (bf16[1088,256]{1,0:T(8,128)(2,1)S(1)}, bf16[1088,256]{1,0:T(8,128)(2,1)S(1)}, u32[]{:S(2)}, u32[]{:S(2)}) collective-permute-start(bf16[1088,256]{1,0:T(8,128)(2,1)S(1)} %collective-permute-done.8.refs_1_), channel_id=1, source_target_pairs={{0,1},{1,64},{64,65},{65,0},{2,3},{3,66},{66,67},{67,2},{4,5},{5,6... | collective-permute-start | bytes 1671176 | tf_op jit(solution)/shard_map/ppermute | solution.py:43
  58.5 3.5 %collective-permute-start.13 = (bf16[1088,256]{1,0:T(8,128)(2,1)S(1)}, bf16[1088,256]{1,0:T(8,128)(2,1)S(1)}, u32[]{:S(2)}, u32[]{:S(2)}) collective-permute-start(bf16[1088,256]{1,0:T(8,128)(2,1)S(1)} %collective-permute-done.10.refs_3_), channel_id=1, source_target_pairs={{0,16},{16,32},{32,48},{48,0},{1,17},{17,33},{33,49},{49,1},{2,18}... | collective-permute-start | bytes 1671176 | tf_op jit(solution)/shard_map/ppermute | solution.py:43
  61.9 0.7 collective-permute-start.14
  62.6 1.7 %collective-permute-start.15 = (bf16[1088,256]{1,0:T(8,128)(2,1)S(1)}, bf16[1088,256]{1,0:T(8,128)(2,1)S(1)}, u32[]{:S(2)}, u32[]{:S(2)}) collective-permute-start(bf16[1088,256]{1,0:T(8,128)(2,1)S(1)} %collective-permute-done.9.refs_2_), channel_id=1, source_target_pairs={{0,56},{8,48},{16,8},{24,0},{32,24},{40,16},{48,40},{56,32},{1,57}... | collective-permute-start | bytes 1671176 | tf_op jit(solution)/shard_map/ppermute | solution.py:52
  64.3 12.4 %give.1 = (bf16[528,512]{1,0:T(8,128)(2,1)S(1)}, bf16[8,64,256]{2,1,0:T(8,128)(2,1)S(1)}) custom-call(bf16[16,256]{1,0:T(8,128)(2,1)S(1)} %collective-permute-done.11.nb_ref.note_ref, bf16[512,512]{1,0:T(8,128)(2,1)S(1)} %collective-permute-done.6.qb_ref.q_ref, f32[4096,128]{1,0:T(8,128)S(1)} %get-tuple-element.41.m_in, ...), custom_call_target="tpu_custom_call" | custom-call | flops 8589934592 | bytes 1048576 | tf_op jit(solution)/shard_map/give/pallas_call | solution.py:473
  77.3 1.1 collective-permute-done.15.refs_7_
  78.4 24.4 %own.1 = (f32[2048,128]{1,0:T(8,128)S(1)}, f32[2048,256]{1,0:T(8,128)S(1)}, bf16[8,64,256]{2,1,0:T(8,128)(2,1)S(1)}, s32[1,128]{1,0:T(1,128)S(1)}) custom-call(bf16[16,256]{1,0:T(8,128)(2,1)S(1)} %get-tuple-element.29.na_ref.note_ref, bf16[512,512]{1,0:T(8,128)(2,1)S(1)} %get-tuple-element.30.qa_ref.q_ref, f32[4096,128]{1,0:T(8,128)S(1)} %get-tuple-element.41.m_in, ...), custom_call_target="tpu_custom_call" | custom-call | flops 17179869184 | bytes 1048576 | tf_op jit(solution)/shard_map/own/pallas_call | solution.py:486
  103.4 12.7 %all_to_all.13.x_ref = bf16[4,192,512]{2,1,0:T(8,128)(2,1)S(1)} all-to-all(bf16[4,192,512]{2,1,0:T(8,128)(2,1)S(1)} %merge.1), channel_id=1, replica_groups=mesh['xh'=2,'z'=4,'c'=2,'y'=4,'xl'=2] {'y'}, dimensions={0} | all-to-all | bytes 1572864 | tf_op jit(solution)/shard_map/all_to_all | solution.py:550
  116.1 1.0 finish.1
  (22 shorter events, 1.9 us)
Async XLA Ops:
  18.7 10.5 %collective-permute-start.6 = (bf16[512,512]{1,0:T(8,128)(2,1)S(1)}, bf16[512,512]{1,0:T(8,128)(2,1)S(1)}, u32[]{:S(2)}, u32[]{:S(2)}) collective-permute-start(bf16[512,512]{1,0:T(8,128)(2,1)S(1)} %get-tuple-element.30.qa_ref.q_ref), channel_id=1, source_target_pairs={{0,8},{8,0},{1,9},{9,1},{2,10},{10,2},{3,11},{11,3},{4,12},{12,4},... | collective-permute-start | bytes 1572872 | tf_op jit(solution)/shard_map/ppermute | solution.py:43
  20.9 5.7 %collective-permute-start = (bf16[272,256]{1,0:T(8,128)(2,1)S(1)}, bf16[272,256]{1,0:T(8,128)(2,1)S(1)}, u32[]{:S(2)}, u32[]{:S(2)}) collective-permute-start(bf16[272,256]{1,0:T(8,128)(2,1)S(1)} %get-tuple-element.31.refs_0_), channel_id=1, source_target_pairs={{0,48},{16,0},{32,16},{48,32},{1,49},{17,1},{33,17},{49,33},{2,50}... | collective-permute-start | bytes 417800 | tf_op jit(solution)/shard_map/ppermute | solution.py:43
  20.9 6.3 %collective-permute-start.5 = (bf16[272,256]{1,0:T(8,128)(2,1)S(1)}, bf16[272,256]{1,0:T(8,128)(2,1)S(1)}, u32[]{:S(2)}, u32[]{:S(2)}) collective-permute-start(bf16[272,256]{1,0:T(8,128)(2,1)S(1)} %get-tuple-element.32.refs_4_), channel_id=1, source_target_pairs={{0,1},{1,64},{64,65},{65,0},{2,3},{3,66},{66,67},{67,2},{4,5},{5,6... | collective-permute-start | bytes 417800 | tf_op jit(solution)/shard_map/ppermute | solution.py:43
  21.8 8.7 %collective-permute-start.1 = (bf16[272,256]{1,0:T(8,128)(2,1)S(1)}, bf16[272,256]{1,0:T(8,128)(2,1)S(1)}, u32[]{:S(2)}, u32[]{:S(2)}) collective-permute-start(bf16[272,256]{1,0:T(8,128)(2,1)S(1)} %get-tuple-element.31.refs_0_), channel_id=1, source_target_pairs={{0,32},{16,48},{32,0},{48,16},{1,33},{17,49},{33,1},{49,17},{2,34}... | collective-permute-start | bytes 417800 | tf_op jit(solution)/shard_map/ppermute | solution.py:43
  24.6 7.2 %collective-permute-start.2 = (bf16[272,256]{1,0:T(8,128)(2,1)S(1)}, bf16[272,256]{1,0:T(8,128)(2,1)S(1)}, u32[]{:S(2)}, u32[]{:S(2)}) collective-permute-start(bf16[272,256]{1,0:T(8,128)(2,1)S(1)} %get-tuple-element.31.refs_0_), channel_id=1, source_target_pairs={{0,16},{16,32},{32,48},{48,0},{1,17},{17,33},{33,49},{49,1},{2,18}... | collective-permute-start | bytes 417800 | tf_op jit(solution)/shard_map/ppermute | solution.py:43
  26.6 5.2 %collective-permute-start.3 = (bf16[272,256]{1,0:T(8,128)(2,1)S(1)}, bf16[272,256]{1,0:T(8,128)(2,1)S(1)}, u32[]{:S(2)}, u32[]{:S(2)}) collective-permute-start(bf16[272,256]{1,0:T(8,128)(2,1)S(1)} %get-tuple-element.32.refs_4_), channel_id=1, source_target_pairs={{0,65},{1,0},{64,1},{65,64},{2,67},{3,2},{66,3},{67,66},{4,69},{5,... | collective-permute-start | bytes 417800 | tf_op jit(solution)/shard_map/ppermute | solution.py:43
  27.1 5.4 %collective-permute-start.4 = (bf16[272,256]{1,0:T(8,128)(2,1)S(1)}, bf16[272,256]{1,0:T(8,128)(2,1)S(1)}, u32[]{:S(2)}, u32[]{:S(2)}) collective-permute-start(bf16[272,256]{1,0:T(8,128)(2,1)S(1)} %get-tuple-element.32.refs_4_), channel_id=1, source_target_pairs={{0,64},{1,65},{64,0},{65,1},{2,66},{3,67},{66,2},{67,3},{4,68},{5,... | collective-permute-start | bytes 417800 | tf_op jit(solution)/shard_map/ppermute | solution.py:43
  29.2 12.7 %collective-permute-start.11 = (bf16[16,256]{1,0:T(8,128)(2,1)S(1)}, bf16[16,256]{1,0:T(8,128)(2,1)S(1)}, u32[]{:S(2)}, u32[]{:S(2)}) collective-permute-start(bf16[16,256]{1,0:T(8,128)(2,1)S(1)} %get-tuple-element.29.na_ref.note_ref), channel_id=1, source_target_pairs={{0,8},{8,0},{1,9},{9,1},{2,10},{10,2},{3,11},{11,3},{4,12},{12,4},... | collective-permute-start | bytes 24584 | tf_op jit(solution)/shard_map/ppermute | solution.py:43
  34.1 22.4 %collective-permute-start.7 = (bf16[1088,256]{1,0:T(8,128)(2,1)S(1)}, bf16[1088,256]{1,0:T(8,128)(2,1)S(1)}, u32[]{:S(2)}, u32[]{:S(2)}) collective-permute-start(bf16[1088,256]{1,0:T(8,128)(2,1)S(1)} %get-tuple-element.34.refs_0_), channel_id=1, source_target_pairs={{0,65},{1,0},{64,1},{65,64},{2,67},{3,2},{66,3},{67,66},{4,69},{5,... | collective-permute-start | bytes 1671176 | tf_op jit(solution)/shard_map/ppermute | solution.py:43
  36.0 20.5 %collective-permute-start.8 = (bf16[1088,256]{1,0:T(8,128)(2,1)S(1)}, bf16[1088,256]{1,0:T(8,128)(2,1)S(1)}, u32[]{:S(2)}, u32[]{:S(2)}) collective-permute-start(bf16[1088,256]{1,0:T(8,128)(2,1)S(1)} %get-tuple-element.34.refs_0_), channel_id=1, source_target_pairs={{0,1},{1,64},{64,65},{65,0},{2,3},{3,66},{66,67},{67,2},{4,5},{5,6... | collective-permute-start | bytes 1671176 | tf_op jit(solution)/shard_map/ppermute | solution.py:43
  36.9 19.6 %collective-permute-start.9 = (bf16[1088,256]{1,0:T(8,128)(2,1)S(1)}, bf16[1088,256]{1,0:T(8,128)(2,1)S(1)}, u32[]{:S(2)}, u32[]{:S(2)}) collective-permute-start(bf16[1088,256]{1,0:T(8,128)(2,1)S(1)} %get-tuple-element.35.refs_1_), channel_id=1, source_target_pairs={{0,48},{16,0},{32,16},{48,32},{1,49},{17,1},{33,17},{49,33},{2,50}... | collective-permute-start | bytes 1671176 | tf_op jit(solution)/shard_map/ppermute | solution.py:43
  41.9 14.6 %collective-permute-start.10 = (bf16[1088,256]{1,0:T(8,128)(2,1)S(1)}, bf16[1088,256]{1,0:T(8,128)(2,1)S(1)}, u32[]{:S(2)}, u32[]{:S(2)}) collective-permute-start(bf16[1088,256]{1,0:T(8,128)(2,1)S(1)} %get-tuple-element.35.refs_1_), channel_id=1, source_target_pairs={{0,16},{16,32},{32,48},{48,0},{1,17},{17,33},{33,49},{49,1},{2,18}... | collective-permute-start | bytes 1671176 | tf_op jit(solution)/shard_map/ppermute | solution.py:43
  56.5 20.3 %collective-permute-start.12 = (bf16[1088,256]{1,0:T(8,128)(2,1)S(1)}, bf16[1088,256]{1,0:T(8,128)(2,1)S(1)}, u32[]{:S(2)}, u32[]{:S(2)}) collective-permute-start(bf16[1088,256]{1,0:T(8,128)(2,1)S(1)} %collective-permute-done.8.refs_1_), channel_id=1, source_target_pairs={{0,1},{1,64},{64,65},{65,0},{2,3},{3,66},{66,67},{67,2},{4,5},{5,6... | collective-permute-start | bytes 1671176 | tf_op jit(solution)/shard_map/ppermute | solution.py:43
  58.5 18.8 %collective-permute-start.13 = (bf16[1088,256]{1,0:T(8,128)(2,1)S(1)}, bf16[1088,256]{1,0:T(8,128)(2,1)S(1)}, u32[]{:S(2)}, u32[]{:S(2)}) collective-permute-start(bf16[1088,256]{1,0:T(8,128)(2,1)S(1)} %collective-permute-done.10.refs_3_), channel_id=1, source_target_pairs={{0,16},{16,32},{32,48},{48,0},{1,17},{17,33},{33,49},{49,1},{2,18}... | collective-permute-start | bytes 1671176 | tf_op jit(solution)/shard_map/ppermute | solution.py:43
  61.9 15.4 %collective-permute-start.14 = (bf16[1088,256]{1,0:T(8,128)(2,1)S(1)}, bf16[1088,256]{1,0:T(8,128)(2,1)S(1)}, u32[]{:S(2)}, u32[]{:S(2)}) collective-permute-start(bf16[1088,256]{1,0:T(8,128)(2,1)S(1)} %collective-permute-done.7.refs_0_), channel_id=1, source_target_pairs={{0,73},{8,65},{1,8},{9,0},{64,9},{72,1},{65,72},{73,64},{2,75},{10... | collective-permute-start | bytes 1671176 | tf_op jit(solution)/shard_map/ppermute | solution.py:52
  62.6 15.8 %collective-permute-start.15 = (bf16[1088,256]{1,0:T(8,128)(2,1)S(1)}, bf16[1088,256]{1,0:T(8,128)(2,1)S(1)}, u32[]{:S(2)}, u32[]{:S(2)}) collective-permute-start(bf16[1088,256]{1,0:T(8,128)(2,1)S(1)} %collective-permute-done.9.refs_2_), channel_id=1, source_target_pairs={{0,56},{8,48},{16,8},{24,0},{32,24},{40,16},{48,40},{56,32},{1,57}... | collective-permute-start | bytes 1671176 | tf_op jit(solution)/shard_map/ppermute | solution.py:52
  76.7 26.0 %collective-permute-start.16 = (bf16[528,512]{1,0:T(8,128)(2,1)S(1)}, bf16[528,512]{1,0:T(8,128)(2,1)S(1)}, u32[]{:S(2)}, u32[]{:S(2)}) collective-permute-start(bf16[528,512]{1,0:T(8,128)(2,1)S(1)} %get-tuple-element.51), channel_id=1, source_target_pairs={{0,8},{8,0},{1,9},{9,1},{2,10},{10,2},{3,11},{11,3},{4,12},{12,4},... | collective-permute-start | bytes 1622024 | tf_op jit(solution)/shard_map/ppermute | solution.py:43
  76.8 25.9 %collective-permute-start.17 = (bf16[8,64,256]{2,1,0:T(8,128)(2,1)S(1)}, bf16[8,64,256]{2,1,0:T(8,128)(2,1)S(1)}, u32[]{:S(2)}, u32[]{:S(2)}) collective-permute-start(bf16[8,64,256]{2,1,0:T(8,128)(2,1)S(1)} %get-tuple-element.54), channel_id=1, source_target_pairs={{0,8},{8,0},{1,9},{9,1},{2,10},{10,2},{3,11},{11,3},{4,12},{12,4},... | collective-permute-start | bytes 786440 | tf_op jit(solution)/shard_map/ppermute | solution.py:43
